TPU v7x, 512 devices: a whole 4x4x16 slice. The times are simulated.
512 devices in a mesh: dp: 64 (over z, x), head: 8 (over y, core).
Axes of the slice: x: 4, y: 4, z: 16, core: 2. Of those that a mesh axis runs over, the one named last changes fastest.
Arguments:
- teacher_feat: bfloat16 [16384, 256], P('dp'), may hold values from -8 to 8
- student_feat: bfloat16 [16384, 256], P('dp'), may hold values from -8 to 8
- proto_v: bfloat16 [256, 32768], P('dp', 'head'), may hold values from -8 to 8
Outputs:
- proto_grad: float32 [256, 32768], P('dp', 'head')
- crop_loss: float32 [16384], P('dp')
All inputs are finite; a program needn't handle non-finite values.
Results may differ from a plain program's by a relative error of at most 0.00095.
Values may be sent and summed in bfloat16 or wider, within the bound.
No kernel may reach another device: no remote copies, remote signals or barrier semaphores. Data moves between devices by JAX's collectives and lax.ppermute only.
A program may use at most 64 MiB of HBM per device.

v0:
```python
import jax
import jax.numpy as jnp
from jax import lax
from jax.sharding import PartitionSpec as P

ITERS = 3


teacher_temp = 0.04
student_temp = 0.1


def unit_rows(features):
    widened = features.astype(jnp.float32)
    scale = jnp.sqrt(jnp.sum(widened * widened, axis=1, keepdims=True) + 1e-06)
    return (widened / scale).astype(jnp.bfloat16)


def col_normalize(mass_q, proto_count):
    proto_sums = lax.psum(jnp.sum(mass_q, axis=0), "dp")
    return mass_q / (proto_count * proto_sums)


def row_normalize(mass_q, crop_count):
    row_totals = lax.psum(jnp.sum(mass_q, axis=1), "head")
    return mass_q / (crop_count * row_totals[:, None])


def local(teacher_feat, student_feat, proto_v):
    teacher_unit = unit_rows(teacher_feat)
    student_unit = unit_rows(student_feat)
    all_rows = lax.all_gather(proto_v, "dp", axis=0, tiled=True)
    col_norms = jnp.sqrt(jnp.sum(jnp.square(all_rows.astype(jnp.float32)), axis=0) + 1e-06)
    crop_count = teacher_unit.shape[0] * lax.axis_size("dp")
    proto_count = all_rows.shape[1] * lax.axis_size("head")
    teacher_raw = jnp.dot(teacher_unit, all_rows, preferred_element_type=jnp.float32)
    mass_q = jnp.exp(teacher_raw / (col_norms * teacher_temp))
    student_raw = jnp.dot(student_unit, all_rows, preferred_element_type=jnp.float32)
    student_scores = student_raw / (col_norms * student_temp)
    spread = jnp.exp(student_scores)
    for repeat in range(ITERS - 1):
        mass_q = row_normalize(col_normalize(mass_q, proto_count), crop_count)
    mass_q = col_normalize(mass_q, proto_count)
    assign = crop_count * row_normalize(mass_q, crop_count)
    exp_totals, cross_sums = lax.psum(
        (jnp.sum(spread, axis=1), jnp.sum(assign * student_scores, axis=1)), "head"
    )
    crop_loss = jnp.log(exp_totals) - cross_sums
    score_grad = ((spread / exp_totals[:, None] - assign) / crop_count).astype(jnp.bfloat16)
    partial_grad = (
        lax.dot_general(
            student_unit, score_grad, (((0,), (0,)), ((), ())), preferred_element_type=jnp.float32
        )
        / student_temp
    )
    weight_rows = lax.psum_scatter(partial_grad, "dp", scatter_dimension=0, tiled=True)
    col_dots = lax.psum(jnp.sum(score_grad.astype(jnp.float32) * student_scores, axis=0), "dp")
    normed_rows = proto_v.astype(jnp.float32) / col_norms
    proto_grad = (weight_rows - normed_rows * col_dots) / col_norms
    return (proto_grad, crop_loss)


def solution(mesh):
    return jax.shard_map(
        local,
        mesh=mesh,
        in_specs=(P("dp", None), P("dp", None), P("dp", "head")),
        out_specs=(P("dp", "head"), P("dp")),
        check_vma=False,
    )
```

profile of v0, /device:TPU:8, one launch (start us, length us, event | category | flops | bytes accessed | tf_op | source)
XLA Modules:
  0.0 1347.0 jit_solution(4625325174119149505)
XLA Ops:
  7.2 0.7 all-gather.3.cloned.1.call-update
  8.0 1.0 fusion.15
  9.0 1.0 fusion.13
  10.0 146.3 %all-gather.3.cloned.1.call-done = bf16[64,4,4096]{2,1,0:T(4,128)(2,1)} async-done(((bf16[1,4,4096]{2,1,0:T(4,128)(2,1)}), bf16[64,4,4096]{2,1,0:T(4,128)(2,1)}) %all-gather.3.cloned.1.call-update) | async-done | bytes 2097168 | tf_op jit(solution)/shard_map/all_gather | solution.py:32
  156.3 2.5 reshape.38
  159.3 2.9 fusion.22
  162.3 277.4 %psum.64 = f32[4096]{0:T(1024)S(1)} all-reduce(f32[4096]{0:T(1024)S(1)} %get-tuple-element.12), channel_id=1, replica_groups=mesh['dp'=64,'head'=8] {'dp'}, use_global_device_ids=true, to_apply=%region_6.0 | all-reduce | flops 4096 | bytes 32768 | tf_op jit(solution)/shard_map/psum | solution.py:20
  439.7 2.6 divide_reduce_fusion
  442.2 10.0 psum.65
  452.2 3.0 fusion.9
  455.2 274.0 %psum.66 = f32[4096]{0:T(1024)S(1)} all-reduce(f32[4096]{0:T(1024)S(1)} %fusion.9), channel_id=1, replica_groups=mesh['dp'=64,'head'=8] {'dp'}, use_global_device_ids=true, to_apply=%region_10.0 | all-reduce | flops 4096 | bytes 32768 | tf_op jit(solution)/shard_map/psum | solution.py:20
  729.2 3.1 fusion.10
  732.3 11.9 psum.67
  744.2 3.2 fusion.11
  747.4 274.0 %psum.68 = f32[4096]{0:T(1024)S(1)} all-reduce(f32[4096]{0:T(1024)S(1)} %fusion.11), channel_id=1, replica_groups=mesh['dp'=64,'head'=8] {'dp'}, use_global_device_ids=true, to_apply=%region_14.0 | all-reduce | flops 4096 | bytes 32768 | tf_op jit(solution)/shard_map/psum | solution.py:20
  1021.3 3.4 fusion.12
  1024.8 2.9 exponential_reduce_fusion
  1027.7 12.4 all-reduce.1
  1040.1 5.7 multiply_reduce_fusion
  1045.8 2.8 convolution_multiply_fusion
  1048.6 1.3 dynamic-slice
  1050.5 13.3 psum.71
  1063.8 274.1 %psum.70 = f32[4096]{0:T(1024)S(1)} all-reduce(f32[4096]{0:T(1024)S(1)} %get-tuple-element.3), channel_id=1, replica_groups=mesh['dp'=64,'head'=8] {'dp'}, use_global_device_ids=true, to_apply=%region_19.0 | all-reduce | flops 4096 | bytes 32768 | tf_op jit(solution)/shard_map/psum | solution.py:57
  1338.6 1.6 fusion.19
  (21 shorter events, 1.2 us)
Async XLA Ops:
  7.2 152.2 %copy-start.1 = (bf16[256,256]{1,0:T(8,128)(2,1)S(1)}, bf16[256,256]{1,0:T(8,128)(2,1)}, u32[]{:S(2)}) copy-start(bf16[256,256]{1,0:T(8,128)(2,1)} %param.3) | copy-start | bytes 393220
  7.2 149.1 %all-gather.3.cloned.1.call-start = ((), (), s32[]{:S(2)}) async-start(), calls=%async_computation | async-start | bytes 2129920 | tf_op jit(solution)/shard_map/all_gather | solution.py:32
  7.9 1330.6 %all-reduce.4.cloned.1.call-start = ((), (), s32[]{:S(2)}) async-start(), calls=%async_computation.1 | async-start | bytes 8388608
  744.2 280.6 %copy-start = (bf16[256,256]{1,0:T(8,128)(2,1)S(1)}, bf16[256,256]{1,0:T(8,128)(2,1)}, u32[]{:S(2)}) copy-start(bf16[256,256]{1,0:T(8,128)(2,1)} %param.4) | copy-start | bytes 393220
  1045.7 292.8 %copy-start.2 = (bf16[4,4096]{1,0:T(4,128)(2,1)S(1)}, bf16[4,4096]{1,0:T(4,128)(2,1)}, u32[]{:S(2)}) copy-start(bf16[4,4096]{1,0:T(4,128)(2,1)} %param.5) | copy-start | bytes 98308
Sparse Core Ops, SparseCore 0:
  11.0 145.3 all-gather.2
  1048.7 283.8 all-reduce.3
where the time goes:
time: 1350 us
  blocking collectives  1150 us (85%)
  waiting for transfers between devices  147 us (11%)
  other arithmetic  25.6 us (2%)
  between operations  14.8 us (1%)
    psum x3, blocking collectives, col_normalize(): proto_sums = lax.psum(jnp.sum(mass_q, axis=0), 'dp')  825 us
    psum x1, blocking collectives, local(): lax.psum(jnp.sum(score_grad.astype(jnp.float32) * student_scores, axis=0)...  274 us
    all_gather x1, waiting for transfers between devices, local(): all_rows = lax.all_gather(proto_v, 'dp', axis=0, tiled=True)  146 us
  transfers between devices with their start and end apart: 2, of which 1 were waited for; matrix products, arithmetic and copies ran while one was open for 0% of the time, Pallas kernels for 0%

commit v1 on v0

v1 whole, which is shorter than its diff:
```python
import jax
import jax.numpy as jnp
from jax import lax
from jax.sharding import Mesh, PartitionSpec as P

ITERS = 3
TEACHER_TEMP = 0.04
STUDENT_TEMP = 0.1
WIRE_SCALE = 32.0

Z = ("h", "l")
ZX = ("h", "l", "x")
XYC = ("x", "y", "c")


def unit_rows(features):
    widened = features.astype(jnp.float32)
    scale = jnp.sqrt(jnp.sum(widened * widened, axis=1, keepdims=True) + 1e-06)
    return (widened / scale).astype(jnp.bfloat16)


def z_sum(values):
    return lax.psum(lax.psum(values, "h"), "l")


def gather_head(values):
    copies = jnp.broadcast_to(values[None], (32,) + values.shape)
    return lax.all_to_all(copies, XYC, 0, 0, tiled=True)


def local(teacher_feat, student_feat, proto_v):
    rows_in, cols_in = proto_v.shape
    nx = lax.axis_size("x")
    nz = lax.axis_size("h") * lax.axis_size("l")
    cols = cols_in // nx
    crop_count = teacher_feat.shape[0] * nz * nx
    proto_count = cols * 32

    units = jnp.concatenate([unit_rows(teacher_feat), unit_rows(student_feat)], axis=1)
    units = lax.all_gather(units, "x", axis=0, tiled=True)
    bot = teacher_feat.shape[1]
    teacher_unit, student_unit = units[:, :bot], units[:, bot:]

    quarters = proto_v.reshape(rows_in, nx, cols).transpose(1, 0, 2)
    quarters = jnp.broadcast_to(quarters[None], (nz, nx, rows_in, cols)).reshape(nz * nx, rows_in, cols)
    protos = lax.all_to_all(quarters, ZX, 0, 0, tiled=True).reshape(nz * nx * rows_in, cols)
    widened = protos.astype(jnp.float32)
    col_norms = jnp.sqrt(jnp.sum(widened * widened, axis=0) + 1e-06)

    teacher_raw = jnp.dot(teacher_unit, protos, preferred_element_type=jnp.float32)
    mass = jnp.exp(teacher_raw / (col_norms * TEACHER_TEMP))
    student_raw = jnp.dot(student_unit, protos, preferred_element_type=jnp.float32)
    student_scores = student_raw / (col_norms * STUDENT_TEMP)
    spread = jnp.exp(student_scores)
    exp_part = jnp.sum(spread, axis=1)

    col_scale = 1.0 / (proto_count * z_sum(jnp.sum(mass, axis=0)))
    got = gather_head(jnp.stack([jnp.sum(mass * col_scale, axis=1), exp_part]))
    row_sum, exp_totals = jnp.sum(got, axis=0)
    row_scale = 1.0 / (crop_count * row_sum)
    col_scale = 1.0 / (proto_count * z_sum(jnp.sum(mass * row_scale[:, None], axis=0)))
    got = gather_head(jnp.stack([jnp.sum(mass * col_scale, axis=1), col_norms]))
    row_scale = 1.0 / (crop_count * jnp.sum(got[:, 0], axis=0))
    me = lax.axis_index(("y", "c"))
    norms = lax.dynamic_index_in_dim(got[:, 1].reshape(nx, 8, cols), me, axis=1, keepdims=False).reshape(-1)
    col_scale = 1.0 / (proto_count * z_sum(jnp.sum(mass * row_scale[:, None], axis=0)))
    weighted = mass * col_scale
    got = gather_head(jnp.stack([jnp.sum(weighted, axis=1), jnp.sum(weighted * student_scores, axis=1)]))
    row_sum, cross = jnp.sum(got, axis=0)
    crop_loss = jnp.log(exp_totals) - cross / row_sum
    score_grad = (spread / exp_totals[:, None] - weighted / row_sum[:, None]).astype(jnp.bfloat16)
    grad = lax.dot_general(
        student_unit, score_grad, (((0,), (0,)), ((), ())), preferred_element_type=jnp.float32
    )
    normed = widened / col_norms
    grad = grad - normed * jnp.sum(normed * grad, axis=0)
    wire = (grad * WIRE_SCALE).astype(jnp.float16).reshape(nz * nx, rows_in, cols)
    wire = lax.all_to_all(wire, ZX, 0, 0, tiled=True)
    total = jnp.sum(wire.astype(jnp.float32).reshape(nz, nx, rows_in, cols), axis=0)
    total = total.transpose(1, 0, 2).reshape(rows_in, cols_in)
    proto_grad = total / (norms * (WIRE_SCALE * STUDENT_TEMP * crop_count))
    loss = lax.dynamic_slice_in_dim(crop_loss, lax.axis_index("x") * teacher_feat.shape[0], teacher_feat.shape[0])
    return proto_grad, loss


def solution(mesh):
    fine = Mesh(mesh.devices.reshape(4, 4, 4, 4, 2), ("h", "l", "x", "y", "c"))
    return jax.shard_map(
        local,
        mesh=fine,
        in_specs=(P(ZX, None), P(ZX, None), P(ZX, ("y", "c"))),
        out_specs=(P(ZX, ("y", "c")), P(ZX)),
        check_vma=False,
    )
```

time: 1350 us -> 254 us (0.19)
  the two profiles are of different devices: /device:TPU:8 before, /device:TPU:2 now
where the time goes in v1:
time: 254 us; the launch traced here: 253 us
  blocking collectives  114 us (45%)
  waiting for transfers between devices  64 us (25%)
  starting transfers between devices  28.1 us (11%)
  other arithmetic  18 us (7%)
  between operations  14.2 us (6%)
  matrix products  11.3 us (4%)
  local copies, waits for them, and re-layouts  3.81 us (2%)
    psum x6, blocking collectives, z_sum(): return lax.psum(lax.psum(values, 'h'), 'l')  73.1 us
    all_to_all x3, blocking collectives, gather_head(): return lax.all_to_all(copies, XYC, 0, 0, tiled=True)  40.5 us
    all_to_all x1, waiting for transfers between devices, local(): wire = lax.all_to_all(wire, ZX, 0, 0, tiled=True)  32.4 us
    all_to_all x1, waiting for transfers between devices, local(): lax.all_to_all(quarters, ZX, 0, 0, tiled=True)  28.7 us
    all_to_all x1, starting transfers between devices, local(): lax.all_to_all(quarters, ZX, 0, 0, tiled=True)  18.6 us
    all_to_all x1, starting transfers between devices, local(): wire = lax.all_to_all(wire, ZX, 0, 0, tiled=True)  9.44 us
  transfers between devices with their start and end apart: 3, of which 3 were waited for; matrix products, arithmetic and copies ran while one was open for 2% of the time, Pallas kernels for 0%

profile of v1, /device:TPU:2, one launch (start us, length us, event | category | flops | bytes accessed | tf_op | source)
XLA Modules:
  0.0 253.2 jit_solution(14859371064580556563)
XLA Ops:
  9.0 18.6 %all-to-all-start = ((bf16[64,4,1024]{2,1,0:T(4,128)(2,1)}), bf16[64,4,1024]{2,1,0:T(4,128)(2,1)S(1)}, u32[]{:S(2)}, u32[]{:S(2)}) async-start(bf16[64,4,1024]{2,1,0:T(4,128)(2,1)} %bitcast.1), calls=%async_computation | async-start | bytes 1048576 | tf_op jit(solution)/shard_map/all_to_all | solution.py:46
  27.7 1.0 fusion.4
  28.7 1.0 fusion.6
  29.7 1.1 fusion.5
  31.6 28.7 %all-to-all-done = bf16[64,4,1024]{2,1,0:T(4,128)(2,1)S(1)} async-done(((bf16[64,4,1024]{2,1,0:T(4,128)(2,1)}), bf16[64,4,1024]{2,1,0:T(4,128)(2,1)S(1)}, u32[]{:S(2)}, u32[]{:S(2)}) %all-to-all-start) | async-done | bytes 524320 | tf_op jit(solution)/shard_map/all_to_all | solution.py:46
  60.8 2.9 %all-gather.2.cloned.1.call-done = bf16[1024,512]{1,0:T(8,128)(2,1)} async-done(((bf16[256,512]{1,0:T(8,128)(2,1)}), bf16[1024,512]{1,0:T(8,128)(2,1)}) %all-gather.2.cloned.1.call-update) | async-done | bytes 1048592 | tf_op jit(solution)/shard_map/all_gather | solution.py:40
  63.6 4.0 %fusion.12 = (f32[1024]{0:T(1024)S(1)}, f32[1024,1024]{0,1:T(8,128)}) fusion(f32[1024]{0:T(1024)S(1)} %get-tuple-element.12, bf16[256,1024]{1,0:T(8,128)(2,1)S(1)} %reshape.91, bf16[1024,512]{1,0:T(8,128)(2,1)} %all-gather.2.cloned.1.call-done), kind=kOutput, calls=%fused_computation.50 | convolution fusion | flops 538967040 | bytes 5251072 | tf_op jit(solution)/shard_map/dot_general | solution.py:50
  67.6 16.5 %psum.42 = f32[1024]{0:T(1024)S(1)} all-reduce(f32[1024]{0:T(1024)S(1)} %get-tuple-element.15), channel_id=1, replica_groups=mesh['h'=4,'l'=4,'x'=4,'y'=4,'c'=2] {'h'}, use_global_device_ids=true, to_apply=%region_4.0 | all-reduce | flops 1024 | bytes 8192 | tf_op jit(solution)/shard_map/psum | solution.py:23
  84.1 11.0 %psum.43 = f32[1024]{0:T(1024)S(1)} all-reduce(f32[1024]{0:T(1024)S(1)} %psum.42), channel_id=1, replica_groups=mesh['h'=4,'l'=4,'x'=4,'y'=4,'c'=2] {'l'}, use_global_device_ids=true, to_apply=%region_5.0 | all-reduce | flops 1024 | bytes 8192 | tf_op jit(solution)/shard_map/psum | solution.py:23
  95.2 2.5 %multiply_reduce_fusion.4 = f32[1024]{0:T(1024)S(1)} fusion(f32[1024,1024]{0,1:T(8,128)} %get-tuple-element.16, f32[1024]{0:T(1024)S(1)} %multiply_divide_fusion.3), kind=kLoop, calls=%fused_computation.5 | loop fusion | flops 2096128 | bytes 4202496 | tf_op jit(solution)/shard_map/reduce_sum | solution.py:58
  97.7 3.0 %exponential_reduce_fusion = (f32[1024]{0:T(1024)S(1)}, f32[1024,1024]{0,1:T(8,128)}) fusion(f32[1024]{0:T(1024)S(1)} %get-tuple-element.11, bf16[256,1024]{1,0:T(8,128)(2,1)S(1)} %reshape.91, bf16[1024,512]{1,0:T(8,128)(2,1)S(1)} %copy-done.1), kind=kOutput, calls=%fused_computation.7 | convolution fusion | flops 538967040 | bytes 5251072 | tf_op jit(solution)/shard_map/dot_general | solution.py:52
  100.8 15.6 %all_to_all.25 = f32[32,2,1024]{2,1,0:T(2,128)S(1)} all-to-all(f32[32,2,1024]{2,1,0:T(2,128)S(1)} %broadcast_in_dim.9), channel_id=1, replica_groups=mesh['h'=4,'l'=4,'x'=4,'y'=4,'c'=2] {'x','y','c'}, dimensions={0} | all-to-all | bytes 524288 | tf_op jit(solution)/shard_map/all_to_all | solution.py:28
  116.5 2.5 %multiply_reduce_fusion.3 = f32[1024]{0:T(1024)S(1)} fusion(f32[1024,1024]{0,1:T(8,128)} %get-tuple-element.16, f32[1024]{0:T(1024)S(1)} %bitcast.37), kind=kLoop, calls=%fused_computation.4 | loop fusion | flops 2096128 | bytes 4202496 | tf_op jit(solution)/shard_map/reduce_sum | solution.py:61
  119.1 13.2 %psum.44 = f32[1024]{0:T(1024)S(1)} all-reduce(f32[1024]{0:T(1024)S(1)} %multiply_reduce_fusion.3), channel_id=1, replica_groups=mesh['h'=4,'l'=4,'x'=4,'y'=4,'c'=2] {'h'}, use_global_device_ids=true, to_apply=%region_10.0 | all-reduce | flops 1024 | bytes 8192 | tf_op jit(solution)/shard_map/psum | solution.py:23
  132.2 9.5 %psum.45 = f32[1024]{0:T(1024)S(1)} all-reduce(f32[1024]{0:T(1024)S(1)} %psum.44), channel_id=1, replica_groups=mesh['h'=4,'l'=4,'x'=4,'y'=4,'c'=2] {'l'}, use_global_device_ids=true, to_apply=%region_11.0 | all-reduce | flops 1024 | bytes 8192 | tf_op jit(solution)/shard_map/psum | solution.py:23
  141.8 2.7 %multiply_reduce_fusion.2 = f32[1024]{0:T(1024)S(1)} fusion(f32[1024,1024]{0,1:T(8,128)} %get-tuple-element.16, f32[1024]{0:T(1024)S(1)} %multiply_divide_fusion.2), kind=kLoop, calls=%fused_computation.3 | loop fusion | flops 2096128 | bytes 4202496 | tf_op jit(solution)/shard_map/reduce_sum | solution.py:62
  144.6 12.5 %all_to_all.26 = f32[32,2,1024]{2,1,0:T(2,128)S(1)} all-to-all(f32[32,2,1024]{2,1,0:T(2,128)S(1)} %broadcast_in_dim.10), channel_id=1, replica_groups=mesh['h'=4,'l'=4,'x'=4,'y'=4,'c'=2] {'x','y','c'}, dimensions={0} | all-to-all | bytes 524288 | tf_op jit(solution)/shard_map/all_to_all | solution.py:28
  157.6 12.5 %psum.46 = f32[1024]{0:T(1024)S(1)} all-reduce(f32[1024]{0:T(1024)S(1)} %multiply_reduce_fusion.1), channel_id=1, replica_groups=mesh['h'=4,'l'=4,'x'=4,'y'=4,'c'=2] {'h'}, use_global_device_ids=true, to_apply=%region_15.16 | all-reduce | flops 1024 | bytes 8192 | tf_op jit(solution)/shard_map/psum | solution.py:23
  170.1 10.4 %psum.47 = f32[1024]{0:T(1024)S(1)} all-reduce(f32[1024]{0:T(1024)S(1)} %psum.46), channel_id=1, replica_groups=mesh['h'=4,'l'=4,'x'=4,'y'=4,'c'=2] {'l'}, use_global_device_ids=true, to_apply=%region_16.17 | all-reduce | flops 1024 | bytes 8192 | tf_op jit(solution)/shard_map/psum | solution.py:23
  180.5 4.1 %multiply_reduce_fusion.5 = (f32[1024]{0:T(1024)S(1)}, f32[1024]{0:T(1024)S(1)}) fusion(f32[1024,1024]{0,1:T(8,128)} %get-tuple-element.16, f32[1024]{0:T(1024)S(1)} %multiply_divide_fusion, f32[1024,1024]{0,1:T(8,128)} %get-tuple-element.14), kind=kLoop, calls=%fused_computation.8 | loop fusion | flops 4192256 | bytes 8400896 | tf_op jit(solution)/shard_map/reduce_sum | solution.py:68
  184.7 12.5 %all_to_all.27 = f32[32,2,1024]{2,1,0:T(2,128)S(1)} all-to-all(f32[32,2,1024]{2,1,0:T(2,128)S(1)} %broadcast_in_dim.11), channel_id=1, replica_groups=mesh['h'=4,'l'=4,'x'=4,'y'=4,'c'=2] {'x','y','c'}, dimensions={0} | all-to-all | bytes 524288 | tf_op jit(solution)/shard_map/all_to_all | solution.py:28
  197.2 4.4 %multiply_reduce_fusion.6 = (f32[1024]{0:T(1024)S(1)}, f32[256,1024]{1,0:T(8,128)S(1)}) fusion(bf16[256,1024]{1,0:T(8,128)(2,1)S(1)} %reshape.91, f32[1024]{0:T(1024)S(1)} %get-tuple-element.10, f32[1024,1024]{0,1:T(8,128)} %get-tuple-element.14, f32[1024,1024]{0,1:T(8,128)} %get-tuple-element.16, f32[1024]{0:T(1024)S(1)} %bitcast.34, ...), kind=kOutput, calls=%fused_computation.13 | convolution fusion | flops 543161344 | bytes 10506240 | tf_op jit(solution)/shard_map/dot_general | solution.py:72
  202.8 9.4 %all-to-all-start.4 = ((f16[64,4,1024]{2,1,0:T(4,128)(2,1)}), f16[64,4,1024]{2,1,0:T(4,128)(2,1)S(1)}, u32[]{:S(2)}, u32[]{:S(2)}) async-start(f16[64,4,1024]{2,1,0:T(4,128)(2,1)} %reshape.92), calls=%async_computation.4 | async-start | bytes 1048576 | tf_op jit(solution)/shard_map/all_to_all | solution.py:78
  213.0 32.4 %all-to-all-done.4 = f16[64,4,1024]{2,1,0:T(4,128)(2,1)S(1)} async-done(((f16[64,4,1024]{2,1,0:T(4,128)(2,1)}), f16[64,4,1024]{2,1,0:T(4,128)(2,1)S(1)}, u32[]{:S(2)}, u32[]{:S(2)}) %all-to-all-start.4) | async-done | bytes 524320 | tf_op jit(solution)/shard_map/all_to_all | solution.py:78
  (39 shorter events, 6.9 us)
Async XLA Ops:
  9.0 51.4 %all-to-all-start = ((bf16[64,4,1024]{2,1,0:T(4,128)(2,1)}), bf16[64,4,1024]{2,1,0:T(4,128)(2,1)S(1)}, u32[]{:S(2)}, u32[]{:S(2)}) async-start(bf16[64,4,1024]{2,1,0:T(4,128)(2,1)} %bitcast.1), calls=%async_computation | async-start | bytes 1048576 | tf_op jit(solution)/shard_map/all_to_all | solution.py:46
  27.6 36.0 %all-gather.2.cloned.1.call-start = ((), (), s32[]{:S(2)}) async-start(), calls=%async_computation.5 | async-start | bytes 1310720 | tf_op jit(solution)/shard_map/all_gather | solution.py:40
  67.6 30.1 %copy-start.1 = (bf16[1024,512]{1,0:T(8,128)(2,1)S(1)}, bf16[1024,512]{1,0:T(8,128)(2,1)}, u32[]{:S(2)}) copy-start(bf16[1024,512]{1,0:T(8,128)(2,1)} %all-gather.2.cloned.1.call-done) | copy-start | bytes 3145732
  141.8 15.5 %copy-start = (f32[1024,1024]{0,1:T(8,128)S(1)}, f32[1024,1024]{0,1:T(8,128)}, u32[]{:S(2)}) copy-start(f32[1024,1024]{0,1:T(8,128)} %get-tuple-element.16) | copy-start | bytes 12582916
  202.8 42.6 %all-to-all-start.4 = ((f16[64,4,1024]{2,1,0:T(4,128)(2,1)}), f16[64,4,1024]{2,1,0:T(4,128)(2,1)S(1)}, u32[]{:S(2)}, u32[]{:S(2)}) async-start(f16[64,4,1024]{2,1,0:T(4,128)(2,1)} %reshape.92), calls=%async_computation.4 | async-start | bytes 1048576 | tf_op jit(solution)/shard_map/all_to_all | solution.py:78
Sparse Core Ops, SparseCore 0:
  31.7 31.8 all-gather.1

commit v2 on v1

v2 whole, which is shorter than its diff:
```python
import functools

import jax
import jax.numpy as jnp
from jax import lax
from jax.experimental import pallas as pl
from jax.experimental.pallas import tpu as pltpu
from jax.sharding import Mesh, PartitionSpec as P

ITERS = 3
TEACHER_TEMP = 0.04
STUDENT_TEMP = 0.1
WIRE_SCALE = 32.0

Z = ("h", "l")
ZX = ("h", "l", "x")
XYC = ("x", "y", "c")


def unit_rows(features):
    widened = features.astype(jnp.float32)
    scale = jnp.sqrt(jnp.sum(widened * widened, axis=1, keepdims=True) + 1e-06)
    return (widened / scale).astype(jnp.bfloat16)


def z_sum(values):
    return lax.psum(lax.psum(values, "h"), "l")


def gather(values, axes, size):
    copies = jnp.broadcast_to(values[None], (size,) + values.shape)
    return lax.all_to_all(copies, axes, 0, 0, tiled=True)


def gather_head(values):
    return gather(values, XYC, 32)


TILE = 256
LANES = 128
VMEM_LIMIT = 24 * 1024 * 1024


def lanes_to_rows(row):
    return jnp.transpose(jnp.broadcast_to(row, (LANES, row.shape[1])))


def row_totals(block):
    part = block[:, :LANES]
    for start in range(LANES, block.shape[1], LANES):
        part = part + block[:, start : start + LANES]
    return jnp.sum(jnp.transpose(part), axis=0, keepdims=True)


def teacher_kernel(unit_ref, proto_ref, mass_ref, col_ref, norm_ref):
    protos = proto_ref[...]
    widened = protos.astype(jnp.float32)
    norms = jnp.sqrt(jnp.sum(widened * widened, axis=0, keepdims=True) + 1e-06)
    norm_ref[...] = norms
    inverse = 1.0 / (norms * TEACHER_TEMP)
    col_ref[...] = jnp.zeros_like(col_ref)

    @pl.loop(0, mass_ref.shape[0], step=TILE)
    def _(start):
        rows = pl.ds(pl.multiple_of(start, TILE), TILE)
        raw = jnp.dot(unit_ref[rows, : protos.shape[0]], proto_ref[...], preferred_element_type=jnp.float32)
        mass = jnp.exp(raw * inverse)
        mass_ref[rows, :] = mass
        col_ref[...] += jnp.sum(mass, axis=0, keepdims=True)


def student_kernel(unit_ref, proto_ref, norm_ref, score_ref, spread_ref, total_ref):
    inverse = 1.0 / (norm_ref[...] * STUDENT_TEMP)
    bot = proto_ref.shape[0]

    @pl.loop(0, score_ref.shape[0], step=TILE)
    def _(start):
        rows = pl.ds(pl.multiple_of(start, TILE), TILE)
        raw = jnp.dot(unit_ref[rows, bot:], proto_ref[...], preferred_element_type=jnp.float32)
        scores = raw * inverse
        score_ref[rows, :] = scores
        spread = jnp.exp(scores)
        spread_ref[rows, :] = spread
        total_ref[:, rows] = row_totals(spread)


def row_kernel(proto_count, mass_ref, col_ref, out_ref):
    scale = 1.0 / (proto_count * col_ref[...])

    @pl.loop(0, mass_ref.shape[0], step=LANES)
    def _(start):
        rows = pl.ds(pl.multiple_of(start, LANES), LANES)
        out_ref[:, rows] = row_totals(mass_ref[rows, :] * scale)


def col_kernel(crop_count, mass_ref, row_ref, out_ref):
    scale = 1.0 / (crop_count * row_ref[...])
    out_ref[...] = jnp.zeros_like(out_ref)
    for start in range(0, mass_ref.shape[0], LANES):
        tall = lanes_to_rows(scale[:, start : start + LANES])
        for lane in range(0, mass_ref.shape[1], LANES):
            block = mass_ref[start : start + LANES, lane : lane + LANES] * tall
            out_ref[:, lane : lane + LANES] += jnp.sum(block, axis=0, keepdims=True)


def cross_kernel(proto_count, mass_ref, score_ref, col_ref, out_ref):
    scale = 1.0 / (proto_count * col_ref[...])

    @pl.loop(0, mass_ref.shape[0], step=LANES)
    def _(start):
        rows = pl.ds(pl.multiple_of(start, LANES), LANES)
        weighted = mass_ref[rows, :] * scale
        out_ref[0:1, rows] = row_totals(weighted)
        out_ref[1:2, rows] = row_totals(weighted * score_ref[rows, :])


def grad_kernel(proto_count, unit_ref, proto_ref, norm_ref, mass_ref, spread_ref, col_ref, row_ref, total_ref, out_ref):
    scale = 1.0 / (proto_count * col_ref[...])
    bot = proto_ref.shape[0]
    by_row = 1.0 / row_ref[...]
    by_total = 1.0 / total_ref[...]
    for start in range(0, mass_ref.shape[0], TILE):
        pieces = []
        for lane in range(0, mass_ref.shape[1], LANES):
            cols = slice(lane, lane + LANES)
            rows = slice(start, start + TILE)
            tall_total = lanes_to_rows(by_total[:, rows])
            tall_row = lanes_to_rows(by_row[:, rows])
            target = mass_ref[rows, cols] * scale[:, cols] * tall_row
            pieces.append((spread_ref[rows, cols] * tall_total - target).astype(jnp.bfloat16))
        part = lax.dot_general(
            unit_ref[start : start + TILE, bot:], jnp.concatenate(pieces, axis=1),
            (((0,), (0,)), ((), ())), preferred_element_type=jnp.float32,
        )
        if start == 0:
            out_ref[...] = part
        else:
            out_ref[...] += part
    normed = proto_ref[...].astype(jnp.float32) / norm_ref[...]
    grad = out_ref[...]
    dots = jnp.sum(normed * grad, axis=0, keepdims=True)
    out_ref[...] = (grad - normed * dots) * WIRE_SCALE


def call(kernel, outs, *args, flops=0, reads=0):
    held = [pltpu.with_memory_space_constraint(a, pltpu.VMEM) if pinned else a for a, pinned in args]
    return pl.pallas_call(
        kernel,
        out_shape=[pltpu.VMEM(shape, jnp.float32) if pinned else jax.ShapeDtypeStruct(shape, jnp.float32) for shape, pinned in outs],
        in_specs=[pl.BlockSpec(memory_space=pltpu.VMEM)] * len(args),
        out_specs=[pl.BlockSpec(memory_space=pltpu.VMEM)] * len(outs),
        compiler_params=pltpu.CompilerParams(vmem_limit_bytes=VMEM_LIMIT),
        cost_estimate=pl.CostEstimate(flops=flops, bytes_accessed=reads, transcendentals=0),
    )(*held)


def local(teacher_feat, student_feat, proto_v):
    rows_in, cols_in = proto_v.shape
    nx = lax.axis_size("x")
    nz = lax.axis_size("h") * lax.axis_size("l")
    cols = cols_in // nx
    crop_count = teacher_feat.shape[0] * nz * nx
    proto_count = cols * 32

    units = jnp.concatenate([unit_rows(teacher_feat), unit_rows(student_feat)], axis=1)
    bot = teacher_feat.shape[1]
    here = lax.axis_index("x")
    crops_in = units.shape[0]
    gathered = jnp.zeros((nx * crops_in, 2 * bot), units.dtype)
    for step in range(nx):
        block = lax.ppermute(units, "x", [((i + step) % nx, i) for i in range(nx)]) if step else units
        gathered = lax.dynamic_update_slice(gathered, block, ((here + step) % nx * crops_in, 0))

    quarters = proto_v.reshape(rows_in, nx, cols).transpose(1, 0, 2)
    quarters = lax.all_to_all(quarters, "x", 0, 0, tiled=True).reshape(nx * rows_in, cols)
    protos = gather(quarters, Z, nz).reshape(nz * nx * rows_in, cols)
    crops = nx * crops_in
    whole, line = (crops, cols), (1, cols)
    share = functools.partial(call, reads=4 * crops * cols)
    mass, sums, norms = share(teacher_kernel, [(whole, True), (line, False), (line, False)], (gathered, False), (protos, False))
    scores, spread, exp_part = share(
        student_kernel, [(whole, True), (whole, True), ((1, crops), False)], (gathered, False), (protos, False), (norms, False)
    )
    by_col = functools.partial(row_kernel, float(proto_count))
    by_row = functools.partial(col_kernel, float(crop_count))
    masses = z_sum(sums)
    (part,) = share(by_col, [((1, crops), False)], (mass, True), (masses, False))
    totals = jnp.sum(gather_head(part), axis=0)
    (sums,) = share(by_row, [(line, False)], (mass, True), (totals, False))
    masses = z_sum(sums)
    (part,) = share(by_col, [((1, crops), False)], (mass, True), (masses, False))
    both = jnp.sum(gather_head(jnp.concatenate([part, exp_part])), axis=0)
    exp_totals = both[1:]
    (sums,) = share(by_row, [(line, False)], (mass, True), (both[:1], False))
    masses = z_sum(sums)
    (part,) = share(
        functools.partial(cross_kernel, float(proto_count)), [((2, crops), False)], (mass, True), (scores, True), (masses, False)
    )
    both = jnp.sum(gather_head(part), axis=0)
    totals, cross = both[:1], both[1:]
    crop_loss = (jnp.log(exp_totals) - cross / totals)[0]
    (grad,) = share(
        functools.partial(grad_kernel, float(proto_count)), [((bot, cols), False)],
        (gathered, False), (protos, False), (norms, False), (mass, True), (spread, True),
        (masses, False), (totals, False), (exp_totals, False),
    )
    wire = grad.astype(jnp.float16).reshape(nz, nx * rows_in, cols)
    wire = lax.all_to_all(wire, Z, 0, 0, tiled=True)
    total = jnp.sum(wire.astype(jnp.float32), axis=0)
    total = total / (norms * (WIRE_SCALE * STUDENT_TEMP * crop_count))
    total = lax.all_to_all(total.reshape(nx, rows_in, cols), "x", 0, 0, tiled=True)
    proto_grad = total.transpose(1, 0, 2).reshape(rows_in, cols_in)
    loss = lax.dynamic_slice_in_dim(crop_loss, lax.axis_index("x") * teacher_feat.shape[0], teacher_feat.shape[0])
    return proto_grad, loss


def solution(mesh):
    fine = Mesh(mesh.devices.reshape(4, 4, 4, 4, 2), ("h", "l", "x", "y", "c"))
    return jax.shard_map(
        local,
        mesh=fine,
        in_specs=(P(ZX, None), P(ZX, None), P(ZX, ("y", "c"))),
        out_specs=(P(ZX, ("y", "c")), P(ZX)),
        check_vma=False,
    )
```

time: 254 us -> 242 us (0.953)
  the two profiles are of different devices: /device:TPU:2 before, /device:TPU:32 now
where the time goes in v2:
time: 242 us; the launch traced here: 241 us
  blocking collectives  106 us (44%)
  waiting for transfers between devices  52.5 us (22%)
  starting transfers between devices  41.4 us (17%)
  local copies, waits for them, and re-layouts  25.9 us (11%)
  Pallas kernels  8.12 us (3%)
  other arithmetic  5.69 us (2%)
    psum x6, blocking collectives, z_sum(): return lax.psum(lax.psum(values, 'h'), 'l')  70.2 us
    all_to_all x1, waiting for transfers between devices, local(): wire = lax.all_to_all(wire, Z, 0, 0, tiled=True)  29.8 us
    all_to_all x2, blocking collectives, gather(): return lax.all_to_all(copies, axes, 0, 0, tiled=True)  26.3 us
    unnamed x23, local copies, waits for them, and re-layouts  24 us
    all_to_all x2, starting transfers between devices, gather(): return lax.all_to_all(copies, axes, 0, 0, tiled=True)  21.1 us
    all_to_all x1, blocking collectives, local(): lax.all_to_all(quarters, 'x', 0, 0, tiled=True).reshape(nx * rows_in, cols)  9.75 us
    ppermute x3, waiting for transfers between devices, local(): lax.ppermute(units, 'x', [((i + step) % nx, i) for i in range(nx)])  9.39 us
    all_to_all x1, starting transfers between devices, local(): wire = lax.all_to_all(wire, Z, 0, 0, tiled=True)  8.65 us
  transfers between devices with their start and end apart: 7, of which 7 were waited for; matrix products, arithmetic and copies ran while one was open for 2% of the time, Pallas kernels for 1%

profile of v2, /device:TPU:32, one launch (start us, length us, event | category | flops | bytes accessed | tf_op | source)
XLA Modules:
  0.0 240.8 jit_solution(9312522347435558058)
XLA Ops:
  0.6 9.8 %all_to_all.35 = bf16[4,4,1024]{2,1,0:T(4,128)(2,1)S(1)} all-to-all(bf16[4,4,1024]{2,1,0:T(4,128)(2,1)} %bitcast.18), channel_id=1, replica_groups=mesh['h'=4,'l'=4,'x'=4,'y'=4,'c'=2] {'x'}, dimensions={0} | all-to-all | bytes 65536 | tf_op jit(solution)/shard_map/all_to_all | solution.py:175
  11.2 15.2 %all-to-all-start.1 = ((bf16[16,16,1024]{2,1,0:T(8,128)(2,1)}), bf16[16,16,1024]{2,1,0:T(8,128)(2,1)S(1)}, u32[]{:S(2)}, u32[]{:S(2)}) async-start(bf16[16,16,1024]{2,1,0:T(8,128)(2,1)} %broadcast_in_dim.16), calls=%async_computation.1 | async-start | bytes 1048576 | tf_op jit(solution)/shard_map/all_to_all | solution.py:32
  29.8 3.1 %collective-permute-start = (bf16[256,512]{1,0:T(8,128)(2,1)S(1)}, bf16[256,512]{1,0:T(8,128)(2,1)S(1)}, u32[]{:S(2)}, u32[]{:S(2)}) collective-permute-start(bf16[256,512]{1,0:T(8,128)(2,1)S(1)} %get-tuple-element.14), channel_id=1, source_target_pairs={{8,0},{16,8},{24,16},{0,24},{9,1},{17,9},{25,17},{1,25},{10,2},{18... | collective-permute-start | bytes 786440 | tf_op jit(solution)/shard_map/ppermute | solution.py:171
  32.9 3.4 %collective-permute-start.1 = (bf16[256,512]{1,0:T(8,128)(2,1)S(1)}, bf16[256,512]{1,0:T(8,128)(2,1)S(1)}, u32[]{:S(2)}, u32[]{:S(2)}) collective-permute-start(bf16[256,512]{1,0:T(8,128)(2,1)S(1)} %get-tuple-element.14), channel_id=1, source_target_pairs={{16,0},{24,8},{0,16},{8,24},{17,1},{25,9},{1,17},{9,25},{18,2},{26... | collective-permute-start | bytes 786440 | tf_op jit(solution)/shard_map/ppermute | solution.py:171
  38.2 2.3 collective-permute-done
  40.6 4.7 %collective-permute-done.1 = bf16[256,512]{1,0:T(8,128)(2,1)S(1)} collective-permute-done((bf16[256,512]{1,0:T(8,128)(2,1)S(1)}, bf16[256,512]{1,0:T(8,128)(2,1)S(1)}, u32[]{:S(2)}, u32[]{:S(2)}) %collective-permute-start.1) | collective-permute-done | bytes 262176 | tf_op jit(solution)/shard_map/ppermute | solution.py:171
  45.3 2.4 collective-permute-done.2
  47.7 6.0 %all-to-all-done.1 = bf16[16,16,1024]{2,1,0:T(8,128)(2,1)S(1)} async-done(((bf16[16,16,1024]{2,1,0:T(8,128)(2,1)}), bf16[16,16,1024]{2,1,0:T(8,128)(2,1)S(1)}, u32[]{:S(2)}, u32[]{:S(2)}) %all-to-all-start.1) | async-done | bytes 524320 | tf_op jit(solution)/shard_map/all_to_all | solution.py:32
  57.0 14.9 %psum.42 = f32[1,1024]{1,0:T(1,128)S(1)} all-reduce(f32[1,1024]{1,0:T(1,128)S(1)} %get-tuple-element.11), channel_id=1, replica_groups=mesh['h'=4,'l'=4,'x'=4,'y'=4,'c'=2] {'h'}, use_global_device_ids=true, to_apply=%region_2.3 | all-reduce | flops 1024 | bytes 8192 | tf_op jit(solution)/shard_map/psum | solution.py:27
  71.9 8.0 %psum.43.col_ref = f32[1,1024]{1,0:T(1,128)S(1)} all-reduce(f32[1,1024]{1,0:T(1,128)S(1)} %psum.42), channel_id=1, replica_groups=mesh['h'=4,'l'=4,'x'=4,'y'=4,'c'=2] {'l'}, use_global_device_ids=true, to_apply=%region_3.4 | all-reduce | flops 1024 | bytes 8192 | tf_op jit(solution)/shard_map/psum | solution.py:27
  80.0 2.2 copy-done.1
  83.8 5.9 %all-to-all-start.2 = ((f32[32,1,1024]{2,1,0:T(1,128)}), f32[32,1,1024]{2,1,0:T(1,128)S(1)}, u32[]{:S(2)}, u32[]{:S(2)}) async-start(f32[32,1,1024]{2,1,0:T(1,128)} %broadcast_in_dim.36), calls=%async_computation.2 | async-start | bytes 262144 | tf_op jit(solution)/shard_map/all_to_all | solution.py:32
  95.3 2.3 all-to-all-done.2
  100.3 12.0 %psum.44 = f32[1,1024]{1,0:T(1,128)S(1)} all-reduce(f32[1,1024]{1,0:T(1,128)S(1)} %shard_map.53), channel_id=1, replica_groups=mesh['h'=4,'l'=4,'x'=4,'y'=4,'c'=2] {'h'}, use_global_device_ids=true, to_apply=%region_5.6 | all-reduce | flops 1024 | bytes 8192 | tf_op jit(solution)/shard_map/psum | solution.py:27
  112.3 11.7 %psum.45.col_ref = f32[1,1024]{1,0:T(1,128)S(1)} all-reduce(f32[1,1024]{1,0:T(1,128)S(1)} %psum.44), channel_id=1, replica_groups=mesh['h'=4,'l'=4,'x'=4,'y'=4,'c'=2] {'l'}, use_global_device_ids=true, to_apply=%region_6.7 | all-reduce | flops 1024 | bytes 8192 | tf_op jit(solution)/shard_map/psum | solution.py:27
  124.0 2.2 copy-done.3
  127.3 13.8 %all_to_all.36 = f32[32,2,1024]{2,1,0:T(2,128)S(1)} all-to-all(f32[32,2,1024]{2,1,0:T(2,128)S(1)} %broadcast_in_dim.37), channel_id=1, replica_groups=mesh['h'=4,'l'=4,'x'=4,'y'=4,'c'=2] {'x','y','c'}, dimensions={0} | all-to-all | bytes 524288 | tf_op jit(solution)/shard_map/all_to_all | solution.py:32
  143.8 15.2 %psum.46 = f32[1,1024]{1,0:T(1,128)S(1)} all-reduce(f32[1,1024]{1,0:T(1,128)S(1)} %shard_map.55), channel_id=1, replica_groups=mesh['h'=4,'l'=4,'x'=4,'y'=4,'c'=2] {'h'}, use_global_device_ids=true, to_apply=%region_8.9 | all-reduce | flops 1024 | bytes 8192 | tf_op jit(solution)/shard_map/psum | solution.py:27
  158.9 8.4 %psum.47.col_ref = f32[1,1024]{1,0:T(1,128)S(1)} all-reduce(f32[1,1024]{1,0:T(1,128)S(1)} %psum.46), channel_id=1, replica_groups=mesh['h'=4,'l'=4,'x'=4,'y'=4,'c'=2] {'l'}, use_global_device_ids=true, to_apply=%region_9.10 | all-reduce | flops 1024 | bytes 8192 | tf_op jit(solution)/shard_map/psum | solution.py:27
  172.9 12.5 %all_to_all.37 = f32[32,2,1024]{2,1,0:T(2,128)S(1)} all-to-all(f32[32,2,1024]{2,1,0:T(2,128)S(1)} %broadcast_in_dim.38), channel_id=1, replica_groups=mesh['h'=4,'l'=4,'x'=4,'y'=4,'c'=2] {'x','y','c'}, dimensions={0} | all-to-all | bytes 524288 | tf_op jit(solution)/shard_map/all_to_all | solution.py:32
  192.1 8.7 %all-to-all-start.5 = ((f16[16,16,1024]{2,1,0:T(8,128)(2,1)}), f16[16,16,1024]{2,1,0:T(8,128)(2,1)S(1)}, u32[]{:S(2)}, u32[]{:S(2)}) async-start(f16[16,16,1024]{2,1,0:T(8,128)(2,1)} %bitcast.5), calls=%async_computation.5 | async-start | bytes 1048576 | tf_op jit(solution)/shard_map/all_to_all | solution.py:208
  200.8 29.8 %all-to-all-done.5 = f16[16,16,1024]{2,1,0:T(8,128)(2,1)S(1)} async-done(((f16[16,16,1024]{2,1,0:T(8,128)(2,1)}), f16[16,16,1024]{2,1,0:T(8,128)(2,1)S(1)}, u32[]{:S(2)}, u32[]{:S(2)}) %all-to-all-start.5) | async-done | bytes 524320 | tf_op jit(solution)/shard_map/all_to_all | solution.py:208
  231.3 3.3 %all-to-all-start.6 = ((f32[4,4,1024]{2,1,0:T(4,128)}), f32[4,4,1024]{2,1,0:T(4,128)S(1)}, u32[]{:S(2)}, u32[]{:S(2)}) async-start(f32[4,4,1024]{2,1,0:T(4,128)} %broadcast_divide_fusion), calls=%async_computation.6 | async-start | bytes 131072 | tf_op jit(solution)/shard_map/all_to_all | solution.py:211
  235.2 5.0 %all-to-all-done.6 = f32[4,4,1024]{2,1,0:T(4,128)S(1)} async-done(((f32[4,4,1024]{2,1,0:T(4,128)}), f32[4,4,1024]{2,1,0:T(4,128)S(1)}, u32[]{:S(2)}, u32[]{:S(2)}) %all-to-all-start.6) | async-done | bytes 65568 | tf_op jit(solution)/shard_map/all_to_all | solution.py:211
  (57 shorter events, 37.2 us)
Async XLA Ops:
  11.2 42.4 %all-to-all-start.1 = ((bf16[16,16,1024]{2,1,0:T(8,128)(2,1)}), bf16[16,16,1024]{2,1,0:T(8,128)(2,1)S(1)}, u32[]{:S(2)}, u32[]{:S(2)}) async-start(bf16[16,16,1024]{2,1,0:T(8,128)(2,1)} %broadcast_in_dim.16), calls=%async_computation.1 | async-start | bytes 1048576 | tf_op jit(solution)/shard_map/all_to_all | solution.py:32
  29.8 10.8 %collective-permute-start = (bf16[256,512]{1,0:T(8,128)(2,1)S(1)}, bf16[256,512]{1,0:T(8,128)(2,1)S(1)}, u32[]{:S(2)}, u32[]{:S(2)}) collective-permute-start(bf16[256,512]{1,0:T(8,128)(2,1)S(1)} %get-tuple-element.14), channel_id=1, source_target_pairs={{8,0},{16,8},{24,16},{0,24},{9,1},{17,9},{25,17},{1,25},{10,2},{18... | collective-permute-start | bytes 786440 | tf_op jit(solution)/shard_map/ppermute | solution.py:171
  32.9 12.4 %collective-permute-start.1 = (bf16[256,512]{1,0:T(8,128)(2,1)S(1)}, bf16[256,512]{1,0:T(8,128)(2,1)S(1)}, u32[]{:S(2)}, u32[]{:S(2)}) collective-permute-start(bf16[256,512]{1,0:T(8,128)(2,1)S(1)} %get-tuple-element.14), channel_id=1, source_target_pairs={{16,0},{24,8},{0,16},{8,24},{17,1},{25,9},{1,17},{9,25},{18,2},{26... | collective-permute-start | bytes 786440 | tf_op jit(solution)/shard_map/ppermute | solution.py:171
  36.2 11.4 %collective-permute-start.2 = (bf16[256,512]{1,0:T(8,128)(2,1)S(1)}, bf16[256,512]{1,0:T(8,128)(2,1)S(1)}, u32[]{:S(2)}, u32[]{:S(2)}) collective-permute-start(bf16[256,512]{1,0:T(8,128)(2,1)S(1)} %get-tuple-element.14), channel_id=1, source_target_pairs={{24,0},{0,8},{8,16},{16,24},{25,1},{1,9},{9,17},{17,25},{26,2},{2,... | collective-permute-start | bytes 786440 | tf_op jit(solution)/shard_map/ppermute | solution.py:171
  55.1 1.9 copy-start
  80.0 2.2 copy-start.1
  83.8 13.8 %all-to-all-start.2 = ((f32[32,1,1024]{2,1,0:T(1,128)}), f32[32,1,1024]{2,1,0:T(1,128)S(1)}, u32[]{:S(2)}, u32[]{:S(2)}) async-start(f32[32,1,1024]{2,1,0:T(1,128)} %broadcast_in_dim.36), calls=%async_computation.2 | async-start | bytes 262144 | tf_op jit(solution)/shard_map/all_to_all | solution.py:32
  91.3 2.0 copy-start.7
  93.3 2.0 copy-start.9
  97.7 2.2 copy-start.2
  124.0 2.2 copy-start.3
  141.2 2.2 copy-start.4
  167.3 2.2 copy-start.5
  169.5 2.2 copy-start.10
  185.6 2.2 copy-start.6
  187.8 2.2 copy-start.8
  192.1 38.4 %all-to-all-start.5 = ((f16[16,16,1024]{2,1,0:T(8,128)(2,1)}), f16[16,16,1024]{2,1,0:T(8,128)(2,1)S(1)}, u32[]{:S(2)}, u32[]{:S(2)}) async-start(f16[16,16,1024]{2,1,0:T(8,128)(2,1)} %bitcast.5), calls=%async_computation.5 | async-start | bytes 1048576 | tf_op jit(solution)/shard_map/all_to_all | solution.py:208
  231.3 8.9 %all-to-all-start.6 = ((f32[4,4,1024]{2,1,0:T(4,128)}), f32[4,4,1024]{2,1,0:T(4,128)S(1)}, u32[]{:S(2)}, u32[]{:S(2)}) async-start(f32[4,4,1024]{2,1,0:T(4,128)} %broadcast_divide_fusion), calls=%async_computation.6 | async-start | bytes 131072 | tf_op jit(solution)/shard_map/all_to_all | solution.py:211

commit v3 on v2

v3 whole, which is shorter than its diff:
```python
import functools

import jax
import jax.numpy as jnp
from jax import lax
from jax.experimental import pallas as pl
from jax.experimental.pallas import tpu as pltpu
from jax.sharding import Mesh, PartitionSpec as P

ITERS = 3
TEACHER_TEMP = 0.04
STUDENT_TEMP = 0.1
WIRE_SCALE = 32.0

Z = ("h", "l")
ZX = ("h", "l", "x")
XYC = ("x", "y", "c")


def unit_rows(features):
    widened = features.astype(jnp.float32)
    scale = jnp.sqrt(jnp.sum(widened * widened, axis=1, keepdims=True) + 1e-06)
    return (widened / scale).astype(jnp.bfloat16)


def z_sum(values):
    return lax.psum(lax.psum(values, "h"), "l")


def gather(values, axes, size):
    copies = jnp.broadcast_to(values[None], (size,) + values.shape)
    return lax.all_to_all(copies, axes, 0, 0, tiled=True)


def gather_head(values):
    return gather(values, XYC, 32)


TILE = 256
LANES = 128
VMEM_LIMIT = 16 * 1024 * 1024


def lanes_to_rows(row):
    return jnp.transpose(jnp.broadcast_to(row, (LANES, row.shape[1])))


def row_totals(block):
    part = block[:, :LANES]
    for start in range(LANES, block.shape[1], LANES):
        part = part + block[:, start : start + LANES]
    return jnp.sum(jnp.transpose(part), axis=0, keepdims=True)


def masses_of(unit_ref, proto_ref, norm_ref, rows):
    bot = proto_ref.shape[0]
    raw = jnp.dot(unit_ref[rows, :bot], proto_ref[...], preferred_element_type=jnp.float32)
    return jnp.exp(raw * (1.0 / (norm_ref[...] * TEACHER_TEMP)))


def scores_of(unit_ref, proto_ref, norm_ref, rows):
    bot = proto_ref.shape[0]
    raw = jnp.dot(unit_ref[rows, bot:], proto_ref[...], preferred_element_type=jnp.float32)
    return raw * (1.0 / (norm_ref[...] * STUDENT_TEMP))


def teacher_kernel(unit_ref, proto_ref, col_ref, norm_ref):
    widened = proto_ref[...].astype(jnp.float32)
    norm_ref[...] = jnp.sqrt(jnp.sum(widened * widened, axis=0, keepdims=True) + 1e-06)
    col_ref[...] = jnp.zeros_like(col_ref)

    @pl.loop(0, unit_ref.shape[0], step=TILE)
    def _(start):
        rows = pl.ds(pl.multiple_of(start, TILE), TILE)
        col_ref[...] += jnp.sum(masses_of(unit_ref, proto_ref, norm_ref, rows), axis=0, keepdims=True)


def student_kernel(unit_ref, proto_ref, norm_ref, total_ref):
    @pl.loop(0, unit_ref.shape[0], step=TILE)
    def _(start):
        rows = pl.ds(pl.multiple_of(start, TILE), TILE)
        total_ref[:, rows] = row_totals(jnp.exp(scores_of(unit_ref, proto_ref, norm_ref, rows)))


def row_kernel(proto_count, unit_ref, proto_ref, norm_ref, col_ref, out_ref, *mass_ref):
    scale = 1.0 / (proto_count * col_ref[...])

    @pl.loop(0, unit_ref.shape[0], step=TILE)
    def _(start):
        rows = pl.ds(pl.multiple_of(start, TILE), TILE)
        mass = masses_of(unit_ref, proto_ref, norm_ref, rows)
        for ref in mass_ref:
            ref[rows, :] = mass
        out_ref[:, rows] = row_totals(mass * scale)


def col_kernel(crop_count, unit_ref, proto_ref, norm_ref, got_ref, out_ref):
    scale = 1.0 / (crop_count * jnp.sum(got_ref[...], axis=0))
    out_ref[...] = jnp.zeros_like(out_ref)
    for start in range(0, unit_ref.shape[0], TILE):
        tall = lanes_to_rows(scale[:1, start : start + TILE])
        mass = masses_of(unit_ref, proto_ref, norm_ref, slice(start, start + TILE))
        for lane in range(0, mass.shape[1], LANES):
            cols = slice(lane, lane + LANES)
            out_ref[:, cols] += jnp.sum(mass[:, cols] * tall, axis=0, keepdims=True)


def held_col_kernel(crop_count, mass_ref, got_ref, out_ref, both_ref):
    both = jnp.sum(got_ref[...], axis=0)
    both_ref[...] = both
    scale = 1.0 / (crop_count * both)
    out_ref[...] = jnp.zeros_like(out_ref)
    for start in range(0, mass_ref.shape[0], LANES):
        tall = lanes_to_rows(scale[:1, start : start + LANES])
        for lane in range(0, mass_ref.shape[1], LANES):
            block = mass_ref[start : start + LANES, lane : lane + LANES] * tall
            out_ref[:, lane : lane + LANES] += jnp.sum(block, axis=0, keepdims=True)


def cross_kernel(proto_count, unit_ref, proto_ref, norm_ref, col_ref, out_ref, target_ref, score_ref):
    scale = 1.0 / (proto_count * col_ref[...])

    @pl.loop(0, unit_ref.shape[0], step=TILE)
    def _(start):
        rows = pl.ds(pl.multiple_of(start, TILE), TILE)
        scores = scores_of(unit_ref, proto_ref, norm_ref, rows)
        weighted = masses_of(unit_ref, proto_ref, norm_ref, rows) * scale
        score_ref[rows, :] = scores
        target_ref[rows, :] = weighted
        out_ref[0:1, rows] = row_totals(weighted)
        out_ref[1:2, rows] = row_totals(weighted * scores)


def grad_kernel(unit_ref, proto_ref, norm_ref, target_ref, score_ref, got_ref, both_ref, out_ref, loss_ref):
    sums = jnp.sum(got_ref[...], axis=0)
    totals = both_ref[1:2, :]
    loss_ref[...] = jnp.log(totals) - sums[1:2] / sums[0:1]
    bot = proto_ref.shape[0]
    by_row = 1.0 / sums[0:1]
    by_total = 1.0 / totals
    for start in range(0, target_ref.shape[0], TILE):
        rows = slice(start, start + TILE)
        tall_total = lanes_to_rows(by_total[:, rows])
        tall_row = lanes_to_rows(by_row[:, rows])
        pieces = []
        for lane in range(0, target_ref.shape[1], LANES):
            cols = slice(lane, lane + LANES)
            spread = jnp.exp(score_ref[rows, cols]) * tall_total
            pieces.append((spread - target_ref[rows, cols] * tall_row).astype(jnp.bfloat16))
        part = lax.dot_general(
            unit_ref[rows, bot:], jnp.concatenate(pieces, axis=1),
            (((0,), (0,)), ((), ())), preferred_element_type=jnp.float32,
        )
        if start == 0:
            out_ref[...] = part
        else:
            out_ref[...] += part
    normed = proto_ref[...].astype(jnp.float32) / norm_ref[...]
    grad = out_ref[...]
    dots = jnp.sum(normed * grad, axis=0, keepdims=True)
    out_ref[...] = (grad - normed * dots) * WIRE_SCALE


def call(kernel, outs, *args, reads):
    return pl.pallas_call(
        kernel,
        out_shape=[jax.ShapeDtypeStruct(shape, jnp.float32) for shape in outs],
        in_specs=[pl.BlockSpec(memory_space=pltpu.VMEM)] * len(args),
        out_specs=[pl.BlockSpec(memory_space=pltpu.VMEM)] * len(outs),
        compiler_params=pltpu.CompilerParams(vmem_limit_bytes=VMEM_LIMIT),
        cost_estimate=pl.CostEstimate(flops=reads, bytes_accessed=reads, transcendentals=0),
    )(*args)


def local(teacher_feat, student_feat, proto_v):
    rows_in, cols_in = proto_v.shape
    nx = lax.axis_size("x")
    nz = lax.axis_size("h") * lax.axis_size("l")
    cols = cols_in // nx
    crop_count = teacher_feat.shape[0] * nz * nx
    proto_count = cols * 32

    units = jnp.concatenate([unit_rows(teacher_feat), unit_rows(student_feat)], axis=1)
    bot = teacher_feat.shape[1]
    here = lax.axis_index("x")
    crops_in = units.shape[0]
    gathered = jnp.zeros((nx * crops_in, 2 * bot), units.dtype)
    for step in range(nx):
        block = lax.ppermute(units, "x", [((i + step) % nx, i) for i in range(nx)]) if step else units
        gathered = lax.dynamic_update_slice(gathered, block, ((here + step) % nx * crops_in, 0))

    quarters = proto_v.reshape(rows_in, nx, cols).transpose(1, 0, 2)
    quarters = lax.all_to_all(quarters, "x", 0, 0, tiled=True).reshape(nx * rows_in, cols)
    protos = gather(quarters, Z, nz).reshape(nz * nx * rows_in, cols)
    crops = nx * crops_in
    whole, line, tall = (crops, cols), (1, cols), (1, crops)
    share = functools.partial(call, reads=4 * crops * cols)
    by_proto, by_crop = float(proto_count), float(crop_count)
    sums, norms = share(teacher_kernel, [line, line], gathered, protos)
    held = gathered, protos, norms
    (exp_part,) = share(student_kernel, [tall], *held)
    masses = z_sum(sums)
    (part,) = share(functools.partial(row_kernel, by_proto), [tall], *held, masses)
    (sums,) = share(functools.partial(col_kernel, by_crop), [line], *held, gather_head(part))
    masses = z_sum(sums)
    part, mass = share(functools.partial(row_kernel, by_proto), [tall, whole], *held, masses)
    got = gather_head(jnp.concatenate([part, exp_part]))
    sums, both = share(functools.partial(held_col_kernel, by_crop), [line, (2, crops)], mass, got)
    masses = z_sum(sums)
    part, target, scores = share(functools.partial(cross_kernel, by_proto), [(2, crops), whole, whole], *held, masses)
    got = gather_head(part)
    grad, crop_loss = share(grad_kernel, [(bot, cols), tall], *held, target, scores, got, both)
    crop_loss = crop_loss[0]
    wire = grad.astype(jnp.float16).reshape(nz, nx * rows_in, cols)
    wire = lax.all_to_all(wire, Z, 0, 0, tiled=True)
    total = jnp.sum(wire.astype(jnp.float32), axis=0)
    total = total / (norms * (WIRE_SCALE * STUDENT_TEMP * crop_count))
    total = lax.all_to_all(total.reshape(nx, rows_in, cols), "x", 0, 0, tiled=True)
    proto_grad = total.transpose(1, 0, 2).reshape(rows_in, cols_in)
    loss = lax.dynamic_slice_in_dim(crop_loss, lax.axis_index("x") * teacher_feat.shape[0], teacher_feat.shape[0])
    return proto_grad, loss


def solution(mesh):
    fine = Mesh(mesh.devices.reshape(4, 4, 4, 4, 2), ("h", "l", "x", "y", "c"))
    return jax.shard_map(
        local,
        mesh=fine,
        in_specs=(P(ZX, None), P(ZX, None), P(ZX, ("y", "c"))),
        out_specs=(P(ZX, ("y", "c")), P(ZX)),
        check_vma=False,
    )
```

time: 242 us -> 224 us (0.926)
  local copies, waits for them, and re-layouts: 25.9 us -> 3.07 us
  waiting for transfers between devices: 52.5 us -> 56.4 us
  Pallas kernels: 8.12 us -> 12 us
    unnamed x23 -> x1, local copies, waits for them, and re-layouts: 24 us -> 0.63 us
    all_to_all x2, waiting for transfers between devices: 8.32 us -> 12.3 us  [gather(): return lax.all_to_all(copies, axes, 0, 0, tiled=True)]
    pallas_call x8, Pallas kernels: 8.12 us -> 12 us  [call(): pl.pallas_call(kernel, out_shape=[jax.ShapeDtypeStruct(shape, jnp.float32...]
where the time goes in v3:
time: 224 us
  blocking collectives  105 us (47%)
  waiting for transfers between devices  56.4 us (25%)
  starting transfers between devices  41.4 us (18%)
  Pallas kernels  12 us (5%)
  other arithmetic  4.81 us (2%)
  local copies, waits for them, and re-layouts  3.07 us (1%)
    psum x6, blocking collectives, z_sum(): return lax.psum(lax.psum(values, 'h'), 'l')  70.2 us
    all_to_all x1, waiting for transfers between devices, local(): wire = lax.all_to_all(wire, Z, 0, 0, tiled=True)  29.8 us
    all_to_all x2, blocking collectives, gather(): return lax.all_to_all(copies, axes, 0, 0, tiled=True)  24.9 us
    all_to_all x2, starting transfers between devices, gather(): return lax.all_to_all(copies, axes, 0, 0, tiled=True)  21.1 us
    all_to_all x2, waiting for transfers between devices, gather(): return lax.all_to_all(copies, axes, 0, 0, tiled=True)  12.3 us
    pallas_call x8, Pallas kernels, call(): pl.pallas_call(kernel, out_shape=[jax.ShapeDtypeStruct(shape, jnp.float32...  12 us
    all_to_all x1, blocking collectives, local(): lax.all_to_all(quarters, 'x', 0, 0, tiled=True).reshape(nx * rows_in, cols)  9.75 us
    ppermute x3, waiting for transfers between devices, local(): lax.ppermute(units, 'x', [((i + step) % nx, i) for i in range(nx)])  9.39 us
  transfers between devices with their start and end apart: 7, of which 7 were waited for; matrix products, arithmetic and copies ran while one was open for 2% of the time, Pallas kernels for 1%

profile of v3, /device:TPU:32, one launch (start us, length us, event | category | flops | bytes accessed | tf_op | source)
XLA Modules:
  0.0 223.5 jit_solution(11862951947011435106)
XLA Ops:
  0.6 9.8 %all_to_all.35 = bf16[4,4,1024]{2,1,0:T(4,128)(2,1)S(1)} all-to-all(bf16[4,4,1024]{2,1,0:T(4,128)(2,1)} %bitcast.20), channel_id=1, replica_groups=mesh['h'=4,'l'=4,'x'=4,'y'=4,'c'=2] {'x'}, dimensions={0} | all-to-all | bytes 65536 | tf_op jit(solution)/shard_map/all_to_all | solution.py:193
  11.2 15.2 %all-to-all-start.1 = ((bf16[16,16,1024]{2,1,0:T(8,128)(2,1)}), bf16[16,16,1024]{2,1,0:T(8,128)(2,1)S(1)}, u32[]{:S(2)}, u32[]{:S(2)}) async-start(bf16[16,16,1024]{2,1,0:T(8,128)(2,1)} %broadcast_in_dim.16), calls=%async_computation.1 | async-start | bytes 1048576 | tf_op jit(solution)/shard_map/all_to_all | solution.py:32
  29.8 3.1 %collective-permute-start = (bf16[256,512]{1,0:T(8,128)(2,1)S(1)}, bf16[256,512]{1,0:T(8,128)(2,1)S(1)}, u32[]{:S(2)}, u32[]{:S(2)}) collective-permute-start(bf16[256,512]{1,0:T(8,128)(2,1)S(1)} %get-tuple-element.24), channel_id=1, source_target_pairs={{8,0},{16,8},{24,16},{0,24},{9,1},{17,9},{25,17},{1,25},{10,2},{18... | collective-permute-start | bytes 786440 | tf_op jit(solution)/shard_map/ppermute | solution.py:189
  32.9 3.4 %collective-permute-start.1 = (bf16[256,512]{1,0:T(8,128)(2,1)S(1)}, bf16[256,512]{1,0:T(8,128)(2,1)S(1)}, u32[]{:S(2)}, u32[]{:S(2)}) collective-permute-start(bf16[256,512]{1,0:T(8,128)(2,1)S(1)} %get-tuple-element.24), channel_id=1, source_target_pairs={{16,0},{24,8},{0,16},{8,24},{17,1},{25,9},{1,17},{9,25},{18,2},{26... | collective-permute-start | bytes 786440 | tf_op jit(solution)/shard_map/ppermute | solution.py:189
  36.2 1.9 collective-permute-start.2
  38.2 2.3 %collective-permute-done = bf16[256,512]{1,0:T(8,128)(2,1)S(1)} collective-permute-done((bf16[256,512]{1,0:T(8,128)(2,1)S(1)}, bf16[256,512]{1,0:T(8,128)(2,1)S(1)}, u32[]{:S(2)}, u32[]{:S(2)}) %collective-permute-start) | collective-permute-done | bytes 262176 | tf_op jit(solution)/shard_map/ppermute | solution.py:189
  40.6 4.7 %collective-permute-done.1 = bf16[256,512]{1,0:T(8,128)(2,1)S(1)} collective-permute-done((bf16[256,512]{1,0:T(8,128)(2,1)S(1)}, bf16[256,512]{1,0:T(8,128)(2,1)S(1)}, u32[]{:S(2)}, u32[]{:S(2)}) %collective-permute-start.1) | collective-permute-done | bytes 262176 | tf_op jit(solution)/shard_map/ppermute | solution.py:189
  45.3 2.4 %collective-permute-done.2 = bf16[256,512]{1,0:T(8,128)(2,1)S(1)} collective-permute-done((bf16[256,512]{1,0:T(8,128)(2,1)S(1)}, bf16[256,512]{1,0:T(8,128)(2,1)S(1)}, u32[]{:S(2)}, u32[]{:S(2)}) %collective-permute-start.2) | collective-permute-done | bytes 262176 | tf_op jit(solution)/shard_map/ppermute | solution.py:189
  47.7 6.0 %all-to-all-done.1 = bf16[16,16,1024]{2,1,0:T(8,128)(2,1)S(1)} async-done(((bf16[16,16,1024]{2,1,0:T(8,128)(2,1)}), bf16[16,16,1024]{2,1,0:T(8,128)(2,1)S(1)}, u32[]{:S(2)}, u32[]{:S(2)}) %all-to-all-start.1) | async-done | bytes 524320 | tf_op jit(solution)/shard_map/all_to_all | solution.py:32
  55.1 15.0 %psum.42 = f32[1,1024]{1,0:T(1,128)S(1)} all-reduce(f32[1,1024]{1,0:T(1,128)S(1)} %get-tuple-element.14), channel_id=1, replica_groups=mesh['h'=4,'l'=4,'x'=4,'y'=4,'c'=2] {'h'}, use_global_device_ids=true, to_apply=%region_2.3 | all-reduce | flops 1024 | bytes 8192 | tf_op jit(solution)/shard_map/psum | solution.py:27
  70.0 8.0 %psum.43.col_ref = f32[1,1024]{1,0:T(1,128)S(1)} all-reduce(f32[1,1024]{1,0:T(1,128)S(1)} %psum.42), channel_id=1, replica_groups=mesh['h'=4,'l'=4,'x'=4,'y'=4,'c'=2] {'l'}, use_global_device_ids=true, to_apply=%region_3.4 | all-reduce | flops 1024 | bytes 8192 | tf_op jit(solution)/shard_map/psum | solution.py:27
  80.5 5.9 %all-to-all-start.2 = ((f32[32,1,1024]{2,1,0:T(1,128)}), f32[32,1,1024]{2,1,0:T(1,128)S(1)}, u32[]{:S(2)}, u32[]{:S(2)}) async-start(f32[32,1,1024]{2,1,0:T(1,128)} %broadcast_in_dim.36), calls=%async_computation.2 | async-start | bytes 262144 | tf_op jit(solution)/shard_map/all_to_all | solution.py:32
  88.0 6.3 %all-to-all-done.2.got_ref = f32[32,1,1024]{2,1,0:T(1,128)S(1)} async-done(((f32[32,1,1024]{2,1,0:T(1,128)}), f32[32,1,1024]{2,1,0:T(1,128)S(1)}, u32[]{:S(2)}, u32[]{:S(2)}) %all-to-all-start.2) | async-done | bytes 131104 | tf_op jit(solution)/shard_map/all_to_all | solution.py:32
  95.5 12.0 %psum.44 = f32[1,1024]{1,0:T(1,128)S(1)} all-reduce(f32[1,1024]{1,0:T(1,128)S(1)} %shard_map.52), channel_id=1, replica_groups=mesh['h'=4,'l'=4,'x'=4,'y'=4,'c'=2] {'h'}, use_global_device_ids=true, to_apply=%region_4.5 | all-reduce | flops 1024 | bytes 8192 | tf_op jit(solution)/shard_map/psum | solution.py:27
  107.5 11.7 %psum.45.col_ref = f32[1,1024]{1,0:T(1,128)S(1)} all-reduce(f32[1,1024]{1,0:T(1,128)S(1)} %psum.44), channel_id=1, replica_groups=mesh['h'=4,'l'=4,'x'=4,'y'=4,'c'=2] {'l'}, use_global_device_ids=true, to_apply=%region_5.6 | all-reduce | flops 1024 | bytes 8192 | tf_op jit(solution)/shard_map/psum | solution.py:27
  121.0 12.4 %all_to_all.36.got_ref = f32[32,2,1024]{2,1,0:T(2,128)S(1)} all-to-all(f32[32,2,1024]{2,1,0:T(2,128)S(1)} %broadcast_in_dim.37), channel_id=1, replica_groups=mesh['h'=4,'l'=4,'x'=4,'y'=4,'c'=2] {'x','y','c'}, dimensions={0} | all-to-all | bytes 524288 | tf_op jit(solution)/shard_map/all_to_all | solution.py:32
  133.8 15.2 %psum.46 = f32[1,1024]{1,0:T(1,128)S(1)} all-reduce(f32[1,1024]{1,0:T(1,128)S(1)} %get-tuple-element.17), channel_id=1, replica_groups=mesh['h'=4,'l'=4,'x'=4,'y'=4,'c'=2] {'h'}, use_global_device_ids=true, to_apply=%region_6.7 | all-reduce | flops 1024 | bytes 8192 | tf_op jit(solution)/shard_map/psum | solution.py:27
  149.0 8.4 %psum.47.col_ref = f32[1,1024]{1,0:T(1,128)S(1)} all-reduce(f32[1,1024]{1,0:T(1,128)S(1)} %psum.46), channel_id=1, replica_groups=mesh['h'=4,'l'=4,'x'=4,'y'=4,'c'=2] {'l'}, use_global_device_ids=true, to_apply=%region_7.8 | all-reduce | flops 1024 | bytes 8192 | tf_op jit(solution)/shard_map/psum | solution.py:27
  157.3 2.6 %shard_map.56 = (f32[2,1024]{1,0:T(2,128)S(1)}, f32[1024,1024]{1,0:T(8,128)S(1)}, f32[1024,1024]{1,0:T(8,128)S(1)}) custom-call(bf16[1024,512]{1,0:T(8,128)(2,1)S(1)} %constant_dynamic-update-slice_fusion.unit_ref, bf16[256,1024]{1,0:T(8,128)(2,1)S(1)} %bitcast.16, f32[1,1024]{1,0:T(1,128)S(1)} %get-tuple-element.13.norm_ref, f32[1,1024]{1,0:T(1,128)S(1)} %psum.47.col_ref), custom_call_target="tpu_custom_call" | custom-call | flops 4194304 | bytes 4194304 | tf_op jit(solution)/shard_map/pallas_call | solution.py:165
  160.0 12.5 %all_to_all.37.got_ref = f32[32,2,1024]{2,1,0:T(2,128)S(1)} all-to-all(f32[32,2,1024]{2,1,0:T(2,128)S(1)} %broadcast_in_dim.38), channel_id=1, replica_groups=mesh['h'=4,'l'=4,'x'=4,'y'=4,'c'=2] {'x','y','c'}, dimensions={0} | all-to-all | bytes 524288 | tf_op jit(solution)/shard_map/all_to_all | solution.py:32
  174.9 8.6 %all-to-all-start.5 = ((f16[16,16,1024]{2,1,0:T(8,128)(2,1)}), f16[16,16,1024]{2,1,0:T(8,128)(2,1)S(1)}, u32[]{:S(2)}, u32[]{:S(2)}) async-start(f16[16,16,1024]{2,1,0:T(8,128)(2,1)} %bitcast.4), calls=%async_computation.5 | async-start | bytes 1048576 | tf_op jit(solution)/shard_map/all_to_all | solution.py:215
  183.5 29.8 %all-to-all-done.5 = f16[16,16,1024]{2,1,0:T(8,128)(2,1)S(1)} async-done(((f16[16,16,1024]{2,1,0:T(8,128)(2,1)}), f16[16,16,1024]{2,1,0:T(8,128)(2,1)S(1)}, u32[]{:S(2)}, u32[]{:S(2)}) %all-to-all-start.5) | async-done | bytes 524320 | tf_op jit(solution)/shard_map/all_to_all | solution.py:215
  214.0 3.3 %all-to-all-start.6 = ((f32[4,4,1024]{2,1,0:T(4,128)}), f32[4,4,1024]{2,1,0:T(4,128)S(1)}, u32[]{:S(2)}, u32[]{:S(2)}) async-start(f32[4,4,1024]{2,1,0:T(4,128)} %broadcast_divide_fusion), calls=%async_computation.6 | async-start | bytes 131072 | tf_op jit(solution)/shard_map/all_to_all | solution.py:218
  217.9 5.0 %all-to-all-done.6 = f32[4,4,1024]{2,1,0:T(4,128)S(1)} async-done(((f32[4,4,1024]{2,1,0:T(4,128)}), f32[4,4,1024]{2,1,0:T(4,128)S(1)}, u32[]{:S(2)}, u32[]{:S(2)}) %all-to-all-start.6) | async-done | bytes 65568 | tf_op jit(solution)/shard_map/all_to_all | solution.py:218
  (30 shorter events, 17.4 us)
Async XLA Ops:
  11.2 42.4 %all-to-all-start.1 = ((bf16[16,16,1024]{2,1,0:T(8,128)(2,1)}), bf16[16,16,1024]{2,1,0:T(8,128)(2,1)S(1)}, u32[]{:S(2)}, u32[]{:S(2)}) async-start(bf16[16,16,1024]{2,1,0:T(8,128)(2,1)} %broadcast_in_dim.16), calls=%async_computation.1 | async-start | bytes 1048576 | tf_op jit(solution)/shard_map/all_to_all | solution.py:32
  29.8 10.8 %collective-permute-start = (bf16[256,512]{1,0:T(8,128)(2,1)S(1)}, bf16[256,512]{1,0:T(8,128)(2,1)S(1)}, u32[]{:S(2)}, u32[]{:S(2)}) collective-permute-start(bf16[256,512]{1,0:T(8,128)(2,1)S(1)} %get-tuple-element.24), channel_id=1, source_target_pairs={{8,0},{16,8},{24,16},{0,24},{9,1},{17,9},{25,17},{1,25},{10,2},{18... | collective-permute-start | bytes 786440 | tf_op jit(solution)/shard_map/ppermute | solution.py:189
  32.9 12.4 %collective-permute-start.1 = (bf16[256,512]{1,0:T(8,128)(2,1)S(1)}, bf16[256,512]{1,0:T(8,128)(2,1)S(1)}, u32[]{:S(2)}, u32[]{:S(2)}) collective-permute-start(bf16[256,512]{1,0:T(8,128)(2,1)S(1)} %get-tuple-element.24), channel_id=1, source_target_pairs={{16,0},{24,8},{0,16},{8,24},{17,1},{25,9},{1,17},{9,25},{18,2},{26... | collective-permute-start | bytes 786440 | tf_op jit(solution)/shard_map/ppermute | solution.py:189
  36.2 11.4 %collective-permute-start.2 = (bf16[256,512]{1,0:T(8,128)(2,1)S(1)}, bf16[256,512]{1,0:T(8,128)(2,1)S(1)}, u32[]{:S(2)}, u32[]{:S(2)}) collective-permute-start(bf16[256,512]{1,0:T(8,128)(2,1)S(1)} %get-tuple-element.24), channel_id=1, source_target_pairs={{24,0},{0,8},{8,16},{16,24},{25,1},{1,9},{9,17},{17,25},{26,2},{2,... | collective-permute-start | bytes 786440 | tf_op jit(solution)/shard_map/ppermute | solution.py:189
  80.5 13.8 %all-to-all-start.2 = ((f32[32,1,1024]{2,1,0:T(1,128)}), f32[32,1,1024]{2,1,0:T(1,128)S(1)}, u32[]{:S(2)}, u32[]{:S(2)}) async-start(f32[32,1,1024]{2,1,0:T(1,128)} %broadcast_in_dim.36), calls=%async_computation.2 | async-start | bytes 262144 | tf_op jit(solution)/shard_map/all_to_all | solution.py:32
  174.9 38.4 %all-to-all-start.5 = ((f16[16,16,1024]{2,1,0:T(8,128)(2,1)}), f16[16,16,1024]{2,1,0:T(8,128)(2,1)S(1)}, u32[]{:S(2)}, u32[]{:S(2)}) async-start(f16[16,16,1024]{2,1,0:T(8,128)(2,1)} %bitcast.4), calls=%async_computation.5 | async-start | bytes 1048576 | tf_op jit(solution)/shard_map/all_to_all | solution.py:215
  214.0 8.9 %all-to-all-start.6 = ((f32[4,4,1024]{2,1,0:T(4,128)}), f32[4,4,1024]{2,1,0:T(4,128)S(1)}, u32[]{:S(2)}, u32[]{:S(2)}) async-start(f32[4,4,1024]{2,1,0:T(4,128)} %broadcast_divide_fusion), calls=%async_computation.6 | async-start | bytes 131072 | tf_op jit(solution)/shard_map/all_to_all | solution.py:218

commit v4 on v3

--- a/solution.py
+++ b/solution.py
@@ -23,10 +23,6 @@
     return (widened / scale).astype(jnp.bfloat16)
 
 
-def z_sum(values):
-    return lax.psum(lax.psum(values, "h"), "l")
-
-
 def gather(values, axes, size):
     copies = jnp.broadcast_to(values[None], (size,) + values.shape)
     return lax.all_to_all(copies, axes, 0, 0, tiled=True)
@@ -64,7 +60,7 @@
     return raw * (1.0 / (norm_ref[...] * STUDENT_TEMP))
 
 
-def teacher_kernel(unit_ref, proto_ref, col_ref, norm_ref):
+def teacher_kernel(unit_ref, proto_ref, col_ref, norm_ref, mass_ref):
     widened = proto_ref[...].astype(jnp.float32)
     norm_ref[...] = jnp.sqrt(jnp.sum(widened * widened, axis=0, keepdims=True) + 1e-06)
     col_ref[...] = jnp.zeros_like(col_ref)
@@ -72,37 +68,28 @@
     @pl.loop(0, unit_ref.shape[0], step=TILE)
     def _(start):
         rows = pl.ds(pl.multiple_of(start, TILE), TILE)
-        col_ref[...] += jnp.sum(masses_of(unit_ref, proto_ref, norm_ref, rows), axis=0, keepdims=True)
-
-
-def student_kernel(unit_ref, proto_ref, norm_ref, total_ref):
+        mass = masses_of(unit_ref, proto_ref, norm_ref, rows)
+        mass_ref[rows, :] = mass
+        col_ref[...] += jnp.sum(mass, axis=0, keepdims=True)
+
+
+def first_row_kernel(proto_count, unit_ref, proto_ref, norm_ref, mass_ref, got_ref, out_ref):
+    scale = 1.0 / (proto_count * jnp.sum(got_ref[...], axis=0))
+
     @pl.loop(0, unit_ref.shape[0], step=TILE)
     def _(start):
         rows = pl.ds(pl.multiple_of(start, TILE), TILE)
-        total_ref[:, rows] = row_totals(jnp.exp(scores_of(unit_ref, proto_ref, norm_ref, rows)))
-
-
-def row_kernel(proto_count, unit_ref, proto_ref, norm_ref, col_ref, out_ref, *mass_ref):
-    scale = 1.0 / (proto_count * col_ref[...])
-
-    @pl.loop(0, unit_ref.shape[0], step=TILE)
-    def _(start):
-        rows = pl.ds(pl.multiple_of(start, TILE), TILE)
-        mass = masses_of(unit_ref, proto_ref, norm_ref, rows)
-        for ref in mass_ref:
-            ref[rows, :] = mass
-        out_ref[:, rows] = row_totals(mass * scale)
-
-
-def col_kernel(crop_count, unit_ref, proto_ref, norm_ref, got_ref, out_ref):
-    scale = 1.0 / (crop_count * jnp.sum(got_ref[...], axis=0))
-    out_ref[...] = jnp.zeros_like(out_ref)
-    for start in range(0, unit_ref.shape[0], TILE):
-        tall = lanes_to_rows(scale[:1, start : start + TILE])
-        mass = masses_of(unit_ref, proto_ref, norm_ref, slice(start, start + TILE))
-        for lane in range(0, mass.shape[1], LANES):
-            cols = slice(lane, lane + LANES)
-            out_ref[:, cols] += jnp.sum(mass[:, cols] * tall, axis=0, keepdims=True)
+        out_ref[0:1, rows] = row_totals(mass_ref[rows, :] * scale)
+        out_ref[1:2, rows] = row_totals(jnp.exp(scores_of(unit_ref, proto_ref, norm_ref, rows)))
+
+
+def row_kernel(proto_count, mass_ref, got_ref, out_ref):
+    scale = 1.0 / (proto_count * jnp.sum(got_ref[...], axis=0))
+
+    @pl.loop(0, mass_ref.shape[0], step=LANES)
+    def _(start):
+        rows = pl.ds(pl.multiple_of(start, LANES), LANES)
+        out_ref[:, rows] = row_totals(mass_ref[rows, :] * scale)
 
 
 def held_col_kernel(crop_count, mass_ref, got_ref, out_ref, both_ref):
@@ -117,24 +104,26 @@
             out_ref[:, lane : lane + LANES] += jnp.sum(block, axis=0, keepdims=True)
 
 
-def cross_kernel(proto_count, unit_ref, proto_ref, norm_ref, col_ref, out_ref, target_ref, score_ref):
-    scale = 1.0 / (proto_count * col_ref[...])
+def cross_kernel(proto_count, unit_ref, proto_ref, norm_ref, mass_ref, got_ref, out_ref, target_ref, score_ref):
+    scale = 1.0 / (proto_count * jnp.sum(got_ref[...], axis=0))
 
     @pl.loop(0, unit_ref.shape[0], step=TILE)
     def _(start):
         rows = pl.ds(pl.multiple_of(start, TILE), TILE)
         scores = scores_of(unit_ref, proto_ref, norm_ref, rows)
-        weighted = masses_of(unit_ref, proto_ref, norm_ref, rows) * scale
+        weighted = mass_ref[rows, :] * scale
         score_ref[rows, :] = scores
         target_ref[rows, :] = weighted
         out_ref[0:1, rows] = row_totals(weighted)
         out_ref[1:2, rows] = row_totals(weighted * scores)
 
 
-def grad_kernel(unit_ref, proto_ref, norm_ref, target_ref, score_ref, got_ref, both_ref, out_ref, loss_ref):
+def grad_kernel(here_ref, unit_ref, proto_ref, norm_ref, target_ref, score_ref, got_ref, both_ref, out_ref, scale_ref, loss_ref, all_ref):
     sums = jnp.sum(got_ref[...], axis=0)
     totals = both_ref[1:2, :]
-    loss_ref[...] = jnp.log(totals) - sums[1:2] / sums[0:1]
+    all_ref[...] = jnp.log(totals) - sums[1:2] / sums[0:1]
+    block = loss_ref.shape[1]
+    loss_ref[...] = all_ref[:, pl.ds(pl.multiple_of(here_ref[0] * block, block), block)]
     bot = proto_ref.shape[0]
     by_row = 1.0 / sums[0:1]
     by_total = 1.0 / totals
@@ -159,14 +148,21 @@
     grad = out_ref[...]
     dots = jnp.sum(normed * grad, axis=0, keepdims=True)
     out_ref[...] = (grad - normed * dots) * WIRE_SCALE
-
-
-def call(kernel, outs, *args, reads):
+    crop_count = target_ref.shape[0] * 16
+    scale_ref[...] = 1.0 / (norm_ref[...] * (WIRE_SCALE * STUDENT_TEMP * crop_count))
+
+
+def call(kernel, outs, *args, reads, scalar=None, scratch=()):
+    vmem = pl.BlockSpec(memory_space=pltpu.VMEM)
+    specs = [vmem] * len(args)
+    if scalar is not None:
+        args, specs = (scalar,) + args, [pl.BlockSpec(memory_space=pltpu.SMEM)] + specs
     return pl.pallas_call(
         kernel,
         out_shape=[jax.ShapeDtypeStruct(shape, jnp.float32) for shape in outs],
-        in_specs=[pl.BlockSpec(memory_space=pltpu.VMEM)] * len(args),
-        out_specs=[pl.BlockSpec(memory_space=pltpu.VMEM)] * len(outs),
+        in_specs=specs,
+        out_specs=[vmem] * len(outs),
+        scratch_shapes=[pltpu.VMEM(shape, jnp.float32) for shape in scratch],
         compiler_params=pltpu.CompilerParams(vmem_limit_bytes=VMEM_LIMIT),
         cost_estimate=pl.CostEstimate(flops=reads, bytes_accessed=reads, transcendentals=0),
     )(*args)
@@ -196,29 +192,28 @@
     whole, line, tall = (crops, cols), (1, cols), (1, crops)
     share = functools.partial(call, reads=4 * crops * cols)
     by_proto, by_crop = float(proto_count), float(crop_count)
-    sums, norms = share(teacher_kernel, [line, line], gathered, protos)
+    sums, norms, mass = share(teacher_kernel, [line, line, whole], gathered, protos)
     held = gathered, protos, norms
-    (exp_part,) = share(student_kernel, [tall], *held)
-    masses = z_sum(sums)
-    (part,) = share(functools.partial(row_kernel, by_proto), [tall], *held, masses)
-    (sums,) = share(functools.partial(col_kernel, by_crop), [line], *held, gather_head(part))
-    masses = z_sum(sums)
-    part, mass = share(functools.partial(row_kernel, by_proto), [tall, whole], *held, masses)
-    got = gather_head(jnp.concatenate([part, exp_part]))
-    sums, both = share(functools.partial(held_col_kernel, by_crop), [line, (2, crops)], mass, got)
-    masses = z_sum(sums)
-    part, target, scores = share(functools.partial(cross_kernel, by_proto), [(2, crops), whole, whole], *held, masses)
+    to_rows, to_cols = functools.partial(row_kernel, by_proto), functools.partial(held_col_kernel, by_crop)
+    (part,) = share(functools.partial(first_row_kernel, by_proto), [(2, crops)], *held, mass, gather(sums, Z, nz))
+    sums, both = share(to_cols, [line, (2, crops)], mass, gather_head(part))
+    (part,) = share(to_rows, [tall], mass, gather(sums, Z, nz))
+    sums, _ = share(to_cols, [line, tall], mass, gather_head(part))
+    part, target, scores = share(
+        functools.partial(cross_kernel, by_proto), [(2, crops), whole, whole], *held, mass, gather(sums, Z, nz)
+    )
     got = gather_head(part)
-    grad, crop_loss = share(grad_kernel, [(bot, cols), tall], *held, target, scores, got, both)
-    crop_loss = crop_loss[0]
+    grad, scale, loss = share(
+        grad_kernel, [(bot, cols), line, (1, crops_in)], *held, target, scores, got, both,
+        scalar=here.astype(jnp.int32).reshape(1), scratch=[tall],
+    )
     wire = grad.astype(jnp.float16).reshape(nz, nx * rows_in, cols)
     wire = lax.all_to_all(wire, Z, 0, 0, tiled=True)
     total = jnp.sum(wire.astype(jnp.float32), axis=0)
-    total = total / (norms * (WIRE_SCALE * STUDENT_TEMP * crop_count))
+    total = total * scale
     total = lax.all_to_all(total.reshape(nx, rows_in, cols), "x", 0, 0, tiled=True)
     proto_grad = total.transpose(1, 0, 2).reshape(rows_in, cols_in)
-    loss = lax.dynamic_slice_in_dim(crop_loss, lax.axis_index("x") * teacher_feat.shape[0], teacher_feat.shape[0])
-    return proto_grad, loss
+    return proto_grad, loss[0]
 
 
 def solution(mesh):

time: 224 us -> 195 us (0.87)
  waiting for transfers between devices: 56.4 us -> 15.4 us
  blocking collectives: 105 us -> 139 us
  starting transfers between devices: 41.4 us -> 23.6 us
  Pallas kernels: 12 us -> 9.54 us
    psum x6 -> x0, blocking collectives: 70.2 us -> none  [z_sum(): return lax.psum(lax.psum(values, 'h'), 'l')]
    all_to_all x2 -> x6, blocking collectives: 24.9 us -> 88.1 us  [gather(): return lax.all_to_all(copies, axes, 0, 0, tiled=True)]
    all_to_all x0 -> x2, blocking collectives: none -> 41.6 us  [the longest x1 33.6 us: local(): wire = lax.all_to_all(wire, Z, 0, 0, tiled=True)]
    all_to_all x2 -> x0, waiting for transfers between devices: 34.8 us -> none  [the longest x1 29.8 us: local(): wire = lax.all_to_all(wire, Z, 0, 0, tiled=True)]
    all_to_all x2 -> x0, starting transfers between devices: 11.9 us -> none  [the longest x1 8.65 us: local(): wire = lax.all_to_all(wire, Z, 0, 0, tiled=True)]
    all_to_all x2 -> x1, waiting for transfers between devices: 12.3 us -> 6 us  [gather(): return lax.all_to_all(copies, axes, 0, 0, tiled=True)]
    all_to_all x2 -> x1, starting transfers between devices: 21.1 us -> 15.2 us  [gather(): return lax.all_to_all(copies, axes, 0, 0, tiled=True)]
    pallas_call x8 -> x7, Pallas kernels: 12 us -> 9.54 us  [call(): pl.pallas_call(kernel, out_shape=[jax.ShapeDtypeStruct(shape, jnp.float32...]
  transfers between devices with their start and end apart: 7 -> 4, of which waited for: 7 -> 4; matrix products, arithmetic and copies ran while one was open for 2% -> 2% of each run, Pallas kernels for 1% -> 0%
where the time goes in v4:
time: 195 us; the launch traced here: 194 us
  blocking collectives  139 us (71%)
  starting transfers between devices  23.6 us (12%)
  waiting for transfers between devices  15.4 us (8%)
  Pallas kernels  9.54 us (5%)
  other arithmetic  3.36 us (2%)
  local copies, waits for them, and re-layouts  1.97 us (1%)
    all_to_all x6, blocking collectives, gather(): return lax.all_to_all(copies, axes, 0, 0, tiled=True)  88.1 us
    all_to_all x1, blocking collectives, local(): wire = lax.all_to_all(wire, Z, 0, 0, tiled=True)  33.6 us
    all_to_all x1, starting transfers between devices, gather(): return lax.all_to_all(copies, axes, 0, 0, tiled=True)  15.2 us
    all_to_all x1, blocking collectives, local(): lax.all_to_all(quarters, 'x', 0, 0, tiled=True).reshape(nx * rows_in, cols)  9.75 us
    pallas_call x7, Pallas kernels, call(): pl.pallas_call(kernel, out_shape=[jax.ShapeDtypeStruct(shape, jnp.float32...  9.54 us
    ppermute x3, waiting for transfers between devices, local(): lax.ppermute(units, 'x', [((i + step) % nx, i) for i in range(nx)])  9.38 us
    ppermute x3, starting transfers between devices, local(): lax.ppermute(units, 'x', [((i + step) % nx, i) for i in range(nx)])  8.37 us
    all_to_all x1, blocking collectives, local(): lax.all_to_all(total.reshape(nx, rows_in, cols), 'x', 0, 0, tiled=True)  8.02 us
  transfers between devices with their start and end apart: 4, of which 4 were waited for; matrix products, arithmetic and copies ran while one was open for 2% of the time, Pallas kernels for 0%

profile of v4, /device:TPU:32, one launch (start us, length us, event | category | flops | bytes accessed | tf_op | source)
XLA Modules:
  0.0 194.2 jit_solution(11597681956847371473)
XLA Ops:
  0.6 9.8 %all_to_all.50 = bf16[4,4,1024]{2,1,0:T(4,128)(2,1)S(1)} all-to-all(bf16[4,4,1024]{2,1,0:T(4,128)(2,1)} %bitcast.26), channel_id=1, replica_groups=mesh['h'=4,'l'=4,'x'=4,'y'=4,'c'=2] {'x'}, dimensions={0} | all-to-all | bytes 65536 | tf_op jit(solution)/shard_map/all_to_all | solution.py:189
  11.2 15.2 %all-to-all-start.1 = ((bf16[16,16,1024]{2,1,0:T(8,128)(2,1)}), bf16[16,16,1024]{2,1,0:T(8,128)(2,1)S(1)}, u32[]{:S(2)}, u32[]{:S(2)}) async-start(bf16[16,16,1024]{2,1,0:T(8,128)(2,1)} %broadcast_in_dim.28), calls=%async_computation.1 | async-start | bytes 1048576 | tf_op jit(solution)/shard_map/all_to_all | solution.py:28
  27.5 1.0 fusion.2
  28.5 1.1 fusion.1
  29.8 3.1 %collective-permute-start = (bf16[256,512]{1,0:T(8,128)(2,1)S(1)}, bf16[256,512]{1,0:T(8,128)(2,1)S(1)}, u32[]{:S(2)}, u32[]{:S(2)}) collective-permute-start(bf16[256,512]{1,0:T(8,128)(2,1)S(1)} %get-tuple-element.26), channel_id=1, source_target_pairs={{8,0},{16,8},{24,16},{0,24},{9,1},{17,9},{25,17},{1,25},{10,2},{18... | collective-permute-start | bytes 786440 | tf_op jit(solution)/shard_map/ppermute | solution.py:185
  32.9 3.4 %collective-permute-start.1 = (bf16[256,512]{1,0:T(8,128)(2,1)S(1)}, bf16[256,512]{1,0:T(8,128)(2,1)S(1)}, u32[]{:S(2)}, u32[]{:S(2)}) collective-permute-start(bf16[256,512]{1,0:T(8,128)(2,1)S(1)} %get-tuple-element.26), channel_id=1, source_target_pairs={{16,0},{24,8},{0,16},{8,24},{17,1},{25,9},{1,17},{9,25},{18,2},{26... | collective-permute-start | bytes 786440 | tf_op jit(solution)/shard_map/ppermute | solution.py:185
  36.2 1.9 collective-permute-start.2
  38.2 2.3 %collective-permute-done = bf16[256,512]{1,0:T(8,128)(2,1)S(1)} collective-permute-done((bf16[256,512]{1,0:T(8,128)(2,1)S(1)}, bf16[256,512]{1,0:T(8,128)(2,1)S(1)}, u32[]{:S(2)}, u32[]{:S(2)}) %collective-permute-start) | collective-permute-done | bytes 262176 | tf_op jit(solution)/shard_map/ppermute | solution.py:185
  40.6 4.7 %collective-permute-done.1 = bf16[256,512]{1,0:T(8,128)(2,1)S(1)} collective-permute-done((bf16[256,512]{1,0:T(8,128)(2,1)S(1)}, bf16[256,512]{1,0:T(8,128)(2,1)S(1)}, u32[]{:S(2)}, u32[]{:S(2)}) %collective-permute-start.1) | collective-permute-done | bytes 262176 | tf_op jit(solution)/shard_map/ppermute | solution.py:185
  45.3 2.4 %collective-permute-done.2 = bf16[256,512]{1,0:T(8,128)(2,1)S(1)} collective-permute-done((bf16[256,512]{1,0:T(8,128)(2,1)S(1)}, bf16[256,512]{1,0:T(8,128)(2,1)S(1)}, u32[]{:S(2)}, u32[]{:S(2)}) %collective-permute-start.2) | collective-permute-done | bytes 262176 | tf_op jit(solution)/shard_map/ppermute | solution.py:185
  47.7 6.0 %all-to-all-done.1 = bf16[16,16,1024]{2,1,0:T(8,128)(2,1)S(1)} async-done(((bf16[16,16,1024]{2,1,0:T(8,128)(2,1)}), bf16[16,16,1024]{2,1,0:T(8,128)(2,1)S(1)}, u32[]{:S(2)}, u32[]{:S(2)}) %all-to-all-start.1) | async-done | bytes 524320 | tf_op jit(solution)/shard_map/all_to_all | solution.py:28
  53.7 1.4 shard_map.50
  55.1 18.4 %all_to_all.51.got_ref = f32[16,1,1024]{2,1,0:T(1,128)S(1)} all-to-all(f32[16,1,1024]{2,1,0:T(1,128)S(1)} %broadcast_in_dim.60), channel_id=1, replica_groups=mesh['h'=4,'l'=4,'x'=4,'y'=4,'c'=2] {'h','l'}, dimensions={0} | all-to-all | bytes 131072 | tf_op jit(solution)/shard_map/all_to_all | solution.py:28
  73.5 1.8 shard_map.51
  75.4 14.4 %all_to_all.52.got_ref = f32[32,2,1024]{2,1,0:T(2,128)S(1)} all-to-all(f32[32,2,1024]{2,1,0:T(2,128)S(1)} %broadcast_in_dim.61), channel_id=1, replica_groups=mesh['h'=4,'l'=4,'x'=4,'y'=4,'c'=2] {'x','y','c'}, dimensions={0} | all-to-all | bytes 524288 | tf_op jit(solution)/shard_map/all_to_all | solution.py:28
  90.3 16.2 %all_to_all.53.got_ref = f32[16,1,1024]{2,1,0:T(1,128)S(1)} all-to-all(f32[16,1,1024]{2,1,0:T(1,128)S(1)} %broadcast_in_dim.63), channel_id=1, replica_groups=mesh['h'=4,'l'=4,'x'=4,'y'=4,'c'=2] {'h','l'}, dimensions={0} | all-to-all | bytes 131072 | tf_op jit(solution)/shard_map/all_to_all | solution.py:28
  107.6 11.2 %all_to_all.54.got_ref = f32[32,1,1024]{2,1,0:T(1,128)S(1)} all-to-all(f32[32,1,1024]{2,1,0:T(1,128)S(1)} %broadcast_in_dim.65), channel_id=1, replica_groups=mesh['h'=4,'l'=4,'x'=4,'y'=4,'c'=2] {'x','y','c'}, dimensions={0} | all-to-all | bytes 262144 | tf_op jit(solution)/shard_map/all_to_all | solution.py:28
  118.8 1.1 shard_map.54
  119.9 15.7 %all_to_all.55.got_ref = f32[16,1,1024]{2,1,0:T(1,128)S(1)} all-to-all(f32[16,1,1024]{2,1,0:T(1,128)S(1)} %broadcast_in_dim.67), channel_id=1, replica_groups=mesh['h'=4,'l'=4,'x'=4,'y'=4,'c'=2] {'h','l'}, dimensions={0} | all-to-all | bytes 131072 | tf_op jit(solution)/shard_map/all_to_all | solution.py:28
  135.6 1.7 shard_map.55
  137.4 12.2 %all_to_all.56.got_ref = f32[32,2,1024]{2,1,0:T(2,128)S(1)} all-to-all(f32[32,2,1024]{2,1,0:T(2,128)S(1)} %broadcast_in_dim.68), channel_id=1, replica_groups=mesh['h'=4,'l'=4,'x'=4,'y'=4,'c'=2] {'x','y','c'}, dimensions={0} | all-to-all | bytes 524288 | tf_op jit(solution)/shard_map/all_to_all | solution.py:28
  149.6 2.1 %shard_map.56 = (f32[256,1024]{1,0:T(8,128)S(1)}, f32[1,1024]{1,0:T(1,128)S(1)}, f32[1,256]{1,0:T(1,128)}) custom-call(s32[1]{0:T(128)} %bitcast.here_ref, bf16[1024,512]{1,0:T(8,128)(2,1)S(1)} %constant_dynamic-update-slice_fusion.unit_ref, bf16[256,1024]{1,0:T(8,128)(2,1)S(1)} %bitcast.18, f32[1,1024]{1,0:T(1,128)S(1)} %get-tuple-element.14.norm_ref, ...), custom_call_target="tpu_custom_call" | custom-call | flops 4194304 | bytes 4194304 | tf_op jit(solution)/shard_map/pallas_call | solution.py:160
  151.8 33.6 %all_to_all.57 = f16[16,16,1024]{2,1,0:T(8,128)(2,1)S(1)} all-to-all(f16[16,16,1024]{2,1,0:T(8,128)(2,1)S(1)} %bitcast.24), channel_id=1, replica_groups=mesh['h'=4,'l'=4,'x'=4,'y'=4,'c'=2] {'h','l'}, dimensions={0} | all-to-all | bytes 1048576 | tf_op jit(solution)/shard_map/all_to_all | solution.py:211
  185.5 8.0 %all_to_all.58 = f32[4,4,1024]{2,1,0:T(4,128)S(1)} all-to-all(f32[4,4,1024]{2,1,0:T(4,128)S(1)} %broadcast_multiply_fusion), channel_id=1, replica_groups=mesh['h'=4,'l'=4,'x'=4,'y'=4,'c'=2] {'x'}, dimensions={0} | all-to-all | bytes 131072 | tf_op jit(solution)/shard_map/all_to_all | solution.py:214
  (23 shorter events, 4.7 us)
Async XLA Ops:
  11.2 42.4 %all-to-all-start.1 = ((bf16[16,16,1024]{2,1,0:T(8,128)(2,1)}), bf16[16,16,1024]{2,1,0:T(8,128)(2,1)S(1)}, u32[]{:S(2)}, u32[]{:S(2)}) async-start(bf16[16,16,1024]{2,1,0:T(8,128)(2,1)} %broadcast_in_dim.28), calls=%async_computation.1 | async-start | bytes 1048576 | tf_op jit(solution)/shard_map/all_to_all | solution.py:28
  29.8 10.8 %collective-permute-start = (bf16[256,512]{1,0:T(8,128)(2,1)S(1)}, bf16[256,512]{1,0:T(8,128)(2,1)S(1)}, u32[]{:S(2)}, u32[]{:S(2)}) collective-permute-start(bf16[256,512]{1,0:T(8,128)(2,1)S(1)} %get-tuple-element.26), channel_id=1, source_target_pairs={{8,0},{16,8},{24,16},{0,24},{9,1},{17,9},{25,17},{1,25},{10,2},{18... | collective-permute-start | bytes 786440 | tf_op jit(solution)/shard_map/ppermute | solution.py:185
  32.9 12.4 %collective-permute-start.1 = (bf16[256,512]{1,0:T(8,128)(2,1)S(1)}, bf16[256,512]{1,0:T(8,128)(2,1)S(1)}, u32[]{:S(2)}, u32[]{:S(2)}) collective-permute-start(bf16[256,512]{1,0:T(8,128)(2,1)S(1)} %get-tuple-element.26), channel_id=1, source_target_pairs={{16,0},{24,8},{0,16},{8,24},{17,1},{25,9},{1,17},{9,25},{18,2},{26... | collective-permute-start | bytes 786440 | tf_op jit(solution)/shard_map/ppermute | solution.py:185
  36.2 11.4 %collective-permute-start.2 = (bf16[256,512]{1,0:T(8,128)(2,1)S(1)}, bf16[256,512]{1,0:T(8,128)(2,1)S(1)}, u32[]{:S(2)}, u32[]{:S(2)}) collective-permute-start(bf16[256,512]{1,0:T(8,128)(2,1)S(1)} %get-tuple-element.26), channel_id=1, source_target_pairs={{24,0},{0,8},{8,16},{16,24},{25,1},{1,9},{9,17},{17,25},{26,2},{2,... | collective-permute-start | bytes 786440 | tf_op jit(solution)/shard_map/ppermute | solution.py:185

commit v5 on v4

v5 whole, which is shorter than its diff:
```python
import functools

import jax
import jax.numpy as jnp
from jax import lax
from jax.experimental import pallas as pl
from jax.experimental.pallas import tpu as pltpu
from jax.sharding import Mesh, PartitionSpec as P

ITERS = 3
TEACHER_TEMP = 0.04
STUDENT_TEMP = 0.1
WIRE_SCALE = 32.0

Z = ("h", "l")
ZX = ("h", "l", "x")
XYC = ("x", "y", "c")


def gather(values, axes, size):
    copies = jnp.broadcast_to(values[None], (size,) + values.shape)
    return lax.all_to_all(copies, axes, 0, 0, tiled=True)


def gather_head(values):
    return gather(values, XYC, 32)


TILE = 256
LANES = 128
VMEM_LIMIT = 16 * 1024 * 1024


def lanes_to_rows(row):
    return jnp.transpose(jnp.broadcast_to(row, (LANES, row.shape[1])))


def row_totals(block):
    part = block[:, :LANES]
    for start in range(LANES, block.shape[1], LANES):
        part = part + block[:, start : start + LANES]
    return jnp.sum(jnp.transpose(part), axis=0, keepdims=True)


def unit_kernel(feat_ref, unit_ref):
    bot = feat_ref.shape[1] // 2
    for half in (slice(0, bot), slice(bot, 2 * bot)):
        widened = feat_ref[:, half].astype(jnp.float32)
        scale = jnp.sqrt(jnp.sum(widened * widened, axis=1, keepdims=True) + 1e-06)
        unit_ref[:, half] = (widened / scale).astype(jnp.bfloat16)


def fold(row):
    return jnp.concatenate([row[:, i : i + LANES] for i in range(0, row.shape[1], LANES)], axis=0)


def unfold(block):
    return jnp.concatenate([block[i : i + 1, :] for i in range(block.shape[0])], axis=1)


def store_totals(out_ref, first, block):
    for i in range(TILE // LANES):
        out_ref[pl.ds(first + i, 1), :] = row_totals(block[i * LANES : (i + 1) * LANES, :])


def masses_of(unit_ref, proto_ref, norm_ref, rows):
    bot = proto_ref.shape[0]
    raw = jnp.dot(unit_ref[rows, :bot], proto_ref[...], preferred_element_type=jnp.float32)
    return jnp.exp(raw * (1.0 / (norm_ref[...] * TEACHER_TEMP)))


def scores_of(unit_ref, proto_ref, norm_ref, rows):
    bot = proto_ref.shape[0]
    raw = jnp.dot(unit_ref[rows, bot:], proto_ref[...], preferred_element_type=jnp.float32)
    return raw * (1.0 / (norm_ref[...] * STUDENT_TEMP))


def teacher_kernel(unit_ref, proto_ref, col_ref, norm_ref, mass_ref):
    widened = proto_ref[...].astype(jnp.float32)
    norm_ref[...] = jnp.sqrt(jnp.sum(widened * widened, axis=0, keepdims=True) + 1e-06)

    def step(i, sums):
        rows = pl.ds(pl.multiple_of(i * TILE, TILE), TILE)
        mass = masses_of(unit_ref, proto_ref, norm_ref, rows)
        mass_ref[rows, :] = mass
        return sums + jnp.sum(mass, axis=0, keepdims=True)

    steps = unit_ref.shape[0] // TILE
    col_ref[...] = fold(lax.fori_loop(0, steps, step, jnp.zeros(norm_ref.shape, jnp.float32)))


def first_row_kernel(proto_count, unit_ref, proto_ref, norm_ref, mass_ref, got_ref, out_ref, score_ref, spread_ref):
    scale = unfold(1.0 / (proto_count * jnp.sum(got_ref[...], axis=0)))
    half = out_ref.shape[0] // 2

    @pl.loop(0, unit_ref.shape[0] // TILE)
    def _(i):
        rows = pl.ds(pl.multiple_of(i * TILE, TILE), TILE)
        first = i * (TILE // LANES)
        store_totals(out_ref, first, mass_ref[rows, :] * scale)
        scores = scores_of(unit_ref, proto_ref, norm_ref, rows)
        spread = jnp.exp(scores)
        score_ref[rows, :] = scores
        spread_ref[rows, :] = spread
        store_totals(out_ref, half + first, spread)


def row_kernel(proto_count, mass_ref, got_ref, out_ref):
    scale = unfold(1.0 / (proto_count * jnp.sum(got_ref[...], axis=0)))

    @pl.loop(0, mass_ref.shape[0] // TILE)
    def _(i):
        rows = pl.ds(pl.multiple_of(i * TILE, TILE), TILE)
        store_totals(out_ref, i * (TILE // LANES), mass_ref[rows, :] * scale)


def col_sums(scale, mass_ref):
    cols = []
    tall = [lanes_to_rows(scale[i : i + 1, :]) for i in range(scale.shape[0])]
    for lane in range(0, mass_ref.shape[1], LANES):
        total = jnp.zeros((1, LANES), jnp.float32)
        for i, factor in enumerate(tall):
            block = mass_ref[i * LANES : (i + 1) * LANES, lane : lane + LANES] * factor
            total = total + jnp.sum(block, axis=0, keepdims=True)
        cols.append(total)
    return jnp.concatenate(cols, axis=0)


def first_col_kernel(crop_count, mass_ref, got_ref, out_ref, total_ref):
    both = jnp.sum(got_ref[...], axis=0)
    half = both.shape[0] // 2
    total_ref[...] = both[half:]
    out_ref[...] = col_sums(1.0 / (crop_count * both[:half]), mass_ref)


def col_kernel(crop_count, mass_ref, got_ref, out_ref):
    out_ref[...] = col_sums(1.0 / (crop_count * jnp.sum(got_ref[...], axis=0)), mass_ref)


def cross_kernel(proto_count, mass_ref, score_ref, got_ref, out_ref, scale_ref):
    scale = unfold(1.0 / (proto_count * jnp.sum(got_ref[...], axis=0)))
    scale_ref[...] = scale
    half = out_ref.shape[0] // 2

    @pl.loop(0, mass_ref.shape[0] // TILE)
    def _(i):
        rows = pl.ds(pl.multiple_of(i * TILE, TILE), TILE)
        first = i * (TILE // LANES)
        weighted = mass_ref[rows, :] * scale
        store_totals(out_ref, first, weighted)
        store_totals(out_ref, half + first, weighted * score_ref[rows, :])


def grad_kernel(crop_count, here_ref, unit_ref, proto_ref, norm_ref, mass_ref, spread_ref, scale_ref, got_ref, total_ref, out_ref, back_ref, loss_ref, all_ref):
    sums = jnp.sum(got_ref[...], axis=0)
    totals = total_ref[...]
    half = totals.shape[0]
    all_ref[...] = jnp.log(totals) - sums[half:] / sums[:half]
    block = loss_ref.shape[0]
    loss_ref[...] = all_ref[pl.ds(here_ref[0] * block, block), :]
    bot = proto_ref.shape[0]
    by_row = 1.0 / sums[:half]
    by_total = 1.0 / totals
    grad = jnp.zeros(out_ref.shape, jnp.float32)
    for start in range(0, mass_ref.shape[0], TILE):
        tiles = []
        for top in range(start, start + TILE, LANES):
            rows, i = slice(top, top + LANES), top // LANES
            tall_total = lanes_to_rows(by_total[i : i + 1, :])
            tall_row = lanes_to_rows(by_row[i : i + 1, :])
            pieces = []
            for lane in range(0, mass_ref.shape[1], LANES):
                cols = slice(lane, lane + LANES)
                target = mass_ref[rows, cols] * scale_ref[:, cols] * tall_row
                pieces.append((spread_ref[rows, cols] * tall_total - target).astype(jnp.bfloat16))
            tiles.append(jnp.concatenate(pieces, axis=1))
        grad = grad + lax.dot_general(
            unit_ref[start : start + TILE, bot:], jnp.concatenate(tiles, axis=0),
            (((0,), (0,)), ((), ())), preferred_element_type=jnp.float32,
        )
    normed = proto_ref[...].astype(jnp.float32) / norm_ref[...]
    dots = jnp.sum(normed * grad, axis=0, keepdims=True)
    out_ref[...] = (grad - normed * dots) * WIRE_SCALE
    back_ref[...] = 1.0 / (norm_ref[...] * (WIRE_SCALE * STUDENT_TEMP * crop_count))


def call(kernel, outs, *args, reads, scalar=None, scratch=(), dtype=jnp.float32):
    vmem = pl.BlockSpec(memory_space=pltpu.VMEM)
    specs = [vmem] * len(args)
    if scalar is not None:
        args, specs = (scalar,) + args, [pl.BlockSpec(memory_space=pltpu.SMEM)] + specs
    return pl.pallas_call(
        kernel,
        out_shape=[jax.ShapeDtypeStruct(shape, dtype) for shape in outs],
        in_specs=specs,
        out_specs=[vmem] * len(outs),
        scratch_shapes=[pltpu.VMEM(shape, jnp.float32) for shape in scratch],
        compiler_params=pltpu.CompilerParams(vmem_limit_bytes=VMEM_LIMIT),
        cost_estimate=pl.CostEstimate(flops=reads, bytes_accessed=reads, transcendentals=0),
    )(*args)


def local(teacher_feat, student_feat, proto_v):
    rows_in, cols_in = proto_v.shape
    nx = lax.axis_size("x")
    nz = lax.axis_size("h") * lax.axis_size("l")
    cols = cols_in // nx
    crop_count = teacher_feat.shape[0] * nz * nx
    proto_count = cols * 32

    crops_in, bot = teacher_feat.shape
    here = lax.axis_index("x")
    feats = jnp.concatenate([teacher_feat, student_feat], axis=1)
    (units,) = call(unit_kernel, [feats.shape], feats, reads=4 * crops_in * bot, dtype=jnp.bfloat16)
    gathered = jnp.zeros((nx * crops_in, 2 * bot), units.dtype)
    for step in range(nx):
        block = lax.ppermute(units, "x", [((i + step) % nx, i) for i in range(nx)]) if step else units
        gathered = lax.dynamic_update_slice(gathered, block, ((here + step) % nx * crops_in, 0))

    quarters = proto_v.reshape(rows_in, nx, cols).transpose(1, 0, 2)
    quarters = lax.all_to_all(quarters, "x", 0, 0, tiled=True).reshape(nx * rows_in, cols)
    protos = gather(quarters, Z, nz).reshape(bot, cols)

    crops = nx * crops_in
    whole, line = (crops, cols), (1, cols)
    col_fold, row_fold, row_pair = (cols // LANES, LANES), (crops // LANES, LANES), (2 * crops // LANES, LANES)
    share = functools.partial(call, reads=4 * crops * cols)
    by_proto, by_crop = float(proto_count), float(crop_count)
    sums, norms, mass = share(teacher_kernel, [col_fold, line, whole], gathered, protos)
    held = gathered, protos, norms
    part, scores, spread = share(
        functools.partial(first_row_kernel, by_proto), [row_pair, whole, whole], *held, mass, gather(sums, Z, nz)
    )
    sums, totals = share(functools.partial(first_col_kernel, by_crop), [col_fold, row_fold], mass, gather_head(part))
    (part,) = share(functools.partial(row_kernel, by_proto), [row_fold], mass, gather(sums, Z, nz))
    (sums,) = share(functools.partial(col_kernel, by_crop), [col_fold], mass, gather_head(part))
    part, scale = share(functools.partial(cross_kernel, by_proto), [row_pair, line], mass, scores, gather(sums, Z, nz))
    grad, back, loss = share(
        functools.partial(grad_kernel, by_crop), [(bot, cols), line, (crops_in // LANES, LANES)], *held, mass, spread, scale, gather_head(part), totals,
        scalar=here.astype(jnp.int32).reshape(1), scratch=[row_fold],
    )
    wire = lax.all_to_all(grad.astype(jnp.float16).reshape(nz, nx * rows_in, cols), Z, 0, 0, tiled=True)
    total = jnp.sum(wire.astype(jnp.float32), axis=0) * back
    total = lax.all_to_all(total.reshape(nx, rows_in, cols), "x", 0, 0, tiled=True)
    return total.transpose(1, 0, 2).reshape(rows_in, cols_in), loss.reshape(crops_in)


def solution(mesh):
    fine = Mesh(mesh.devices.reshape(4, 4, 4, 4, 2), ("h", "l", "x", "y", "c"))
    return jax.shard_map(
        local,
        mesh=fine,
        in_specs=(P(ZX, None), P(ZX, None), P(ZX, ("y", "c"))),
        out_specs=(P(ZX, ("y", "c")), P(ZX)),
        check_vma=False,
    )
```

time: 195 us -> 193 us (0.990)
  other arithmetic: 3.36 us -> 1.15 us
  waiting for transfers between devices: 15.4 us -> 17.4 us
    all_to_all x1, waiting for transfers between devices: 6 us -> 8.12 us  [gather(): return lax.all_to_all(copies, axes, 0, 0, tiled=True)]
    reduce_sum x3 -> x1, other arithmetic: 2.11 us -> 0.08 us  [local(): total = jnp.sum(wire.astype(jnp.float32), axis=0) * back]
    pallas_call x7 -> x8, Pallas kernels: 9.54 us -> 7.73 us  [call(): pl.pallas_call(kernel, out_shape=[jax.ShapeDtypeStruct(shape, dtype) for...]
  transfers between devices with their start and end apart: 4 -> 4, of which waited for: 4 -> 4; matrix products, arithmetic and copies ran while one was open for 2% -> 1% of each run, Pallas kernels for 0% -> 0%
where the time goes in v5:
time: 193 us; the launch traced here: 192 us
  blocking collectives  139 us (72%)
  starting transfers between devices  23.6 us (12%)
  waiting for transfers between devices  17.4 us (9%)
  Pallas kernels  7.73 us (4%)
    all_to_all x6, blocking collectives, gather(): return lax.all_to_all(copies, axes, 0, 0, tiled=True)  88.1 us
    all_to_all x1, blocking collectives, local(): lax.all_to_all(grad.astype(jnp.float16).reshape(nz, nx * rows_in, cols),...  33.6 us
    all_to_all x1, starting transfers between devices, gather(): return lax.all_to_all(copies, axes, 0, 0, tiled=True)  15.2 us
    all_to_all x1, blocking collectives, local(): lax.all_to_all(quarters, 'x', 0, 0, tiled=True).reshape(nx * rows_in, cols)  9.75 us
    ppermute x3, waiting for transfers between devices, local(): lax.ppermute(units, 'x', [((i + step) % nx, i) for i in range(nx)])  9.26 us
    ppermute x3, starting transfers between devices, local(): lax.ppermute(units, 'x', [((i + step) % nx, i) for i in range(nx)])  8.37 us
    all_to_all x1, waiting for transfers between devices, gather(): return lax.all_to_all(copies, axes, 0, 0, tiled=True)  8.12 us
    all_to_all x1, blocking collectives, local(): lax.all_to_all(total.reshape(nx, rows_in, cols), 'x', 0, 0, tiled=True)  8.04 us
  transfers between devices with their start and end apart: 4, of which 4 were waited for; matrix products, arithmetic and copies ran while one was open for 1% of the time, Pallas kernels for 0%

profile of v5, /device:TPU:32, one launch (start us, length us, event | category | flops | bytes accessed | tf_op | source)
XLA Modules:
  0.0 191.9 jit_solution(7120949283821980880)
XLA Ops:
  0.6 9.8 %all_to_all.50 = bf16[4,4,1024]{2,1,0:T(4,128)(2,1)S(1)} all-to-all(bf16[4,4,1024]{2,1,0:T(4,128)(2,1)} %bitcast.17), channel_id=1, replica_groups=mesh['h'=4,'l'=4,'x'=4,'y'=4,'c'=2] {'x'}, dimensions={0} | all-to-all | bytes 65536 | tf_op jit(solution)/shard_map/all_to_all | solution.py:221
  10.4 0.9 broadcast_in_dim.20
  11.3 15.2 %all-to-all-start.1 = ((bf16[16,16,1024]{2,1,0:T(8,128)(2,1)}), bf16[16,16,1024]{2,1,0:T(8,128)(2,1)S(1)}, u32[]{:S(2)}, u32[]{:S(2)}) async-start(bf16[16,16,1024]{2,1,0:T(8,128)(2,1)} %broadcast_in_dim.20), calls=%async_computation.1 | async-start | bytes 1048576 | tf_op jit(solution)/shard_map/all_to_all | solution.py:22
  26.5 1.0 pad_maximum_fusion.feat_ref
  27.6 3.1 %collective-permute-start = (bf16[256,512]{1,0:T(8,128)(2,1)S(1)}, bf16[256,512]{1,0:T(8,128)(2,1)S(1)}, u32[]{:S(2)}, u32[]{:S(2)}) collective-permute-start(bf16[256,512]{1,0:T(8,128)(2,1)S(1)} %shard_map.50), channel_id=1, source_target_pairs={{8,0},{16,8},{24,16},{0,24},{9,1},{17,9},{25,17},{1,25},{10,2},{18... | collective-permute-start | bytes 786440 | tf_op jit(solution)/shard_map/ppermute | solution.py:217
  30.7 3.4 %collective-permute-start.1 = (bf16[256,512]{1,0:T(8,128)(2,1)S(1)}, bf16[256,512]{1,0:T(8,128)(2,1)S(1)}, u32[]{:S(2)}, u32[]{:S(2)}) collective-permute-start(bf16[256,512]{1,0:T(8,128)(2,1)S(1)} %shard_map.50), channel_id=1, source_target_pairs={{16,0},{24,8},{0,16},{8,24},{17,1},{25,9},{1,17},{9,25},{18,2},{26... | collective-permute-start | bytes 786440 | tf_op jit(solution)/shard_map/ppermute | solution.py:217
  34.1 1.9 %collective-permute-start.2 = (bf16[256,512]{1,0:T(8,128)(2,1)S(1)}, bf16[256,512]{1,0:T(8,128)(2,1)S(1)}, u32[]{:S(2)}, u32[]{:S(2)}) collective-permute-start(bf16[256,512]{1,0:T(8,128)(2,1)S(1)} %shard_map.50), channel_id=1, source_target_pairs={{24,0},{0,8},{8,16},{16,24},{25,1},{1,9},{9,17},{17,25},{26,2},{2,... | collective-permute-start | bytes 786440 | tf_op jit(solution)/shard_map/ppermute | solution.py:217
  36.2 2.2 %collective-permute-done = bf16[256,512]{1,0:T(8,128)(2,1)S(1)} collective-permute-done((bf16[256,512]{1,0:T(8,128)(2,1)S(1)}, bf16[256,512]{1,0:T(8,128)(2,1)S(1)}, u32[]{:S(2)}, u32[]{:S(2)}) %collective-permute-start) | collective-permute-done | bytes 262176 | tf_op jit(solution)/shard_map/ppermute | solution.py:217
  38.4 4.7 %collective-permute-done.1 = bf16[256,512]{1,0:T(8,128)(2,1)S(1)} collective-permute-done((bf16[256,512]{1,0:T(8,128)(2,1)S(1)}, bf16[256,512]{1,0:T(8,128)(2,1)S(1)}, u32[]{:S(2)}, u32[]{:S(2)}) %collective-permute-start.1) | collective-permute-done | bytes 262176 | tf_op jit(solution)/shard_map/ppermute | solution.py:217
  43.1 2.4 %collective-permute-done.2 = bf16[256,512]{1,0:T(8,128)(2,1)S(1)} collective-permute-done((bf16[256,512]{1,0:T(8,128)(2,1)S(1)}, bf16[256,512]{1,0:T(8,128)(2,1)S(1)}, u32[]{:S(2)}, u32[]{:S(2)}) %collective-permute-start.2) | collective-permute-done | bytes 262176 | tf_op jit(solution)/shard_map/ppermute | solution.py:217
  45.6 8.1 %all-to-all-done.1 = bf16[16,16,1024]{2,1,0:T(8,128)(2,1)S(1)} async-done(((bf16[16,16,1024]{2,1,0:T(8,128)(2,1)}), bf16[16,16,1024]{2,1,0:T(8,128)(2,1)S(1)}, u32[]{:S(2)}, u32[]{:S(2)}) %all-to-all-start.1) | async-done | bytes 524320 | tf_op jit(solution)/shard_map/all_to_all | solution.py:22
  53.7 1.4 shard_map.51
  55.1 18.4 %all_to_all.51.got_ref = f32[16,8,128]{2,1,0:T(8,128)S(1)} all-to-all(f32[16,8,128]{2,1,0:T(8,128)S(1)} %broadcast_in_dim.21), channel_id=1, replica_groups=mesh['h'=4,'l'=4,'x'=4,'y'=4,'c'=2] {'h','l'}, dimensions={0} | all-to-all | bytes 131072 | tf_op jit(solution)/shard_map/all_to_all | solution.py:22
  73.5 1.8 shard_map.52
  75.3 14.4 %all_to_all.52.got_ref = f32[32,16,128]{2,1,0:T(8,128)S(1)} all-to-all(f32[32,16,128]{2,1,0:T(8,128)S(1)} %broadcast_in_dim.22), channel_id=1, replica_groups=mesh['h'=4,'l'=4,'x'=4,'y'=4,'c'=2] {'x','y','c'}, dimensions={0} | all-to-all | bytes 524288 | tf_op jit(solution)/shard_map/all_to_all | solution.py:22
  90.2 16.2 %all_to_all.53.got_ref = f32[16,8,128]{2,1,0:T(8,128)S(1)} all-to-all(f32[16,8,128]{2,1,0:T(8,128)S(1)} %broadcast_in_dim.23), channel_id=1, replica_groups=mesh['h'=4,'l'=4,'x'=4,'y'=4,'c'=2] {'h','l'}, dimensions={0} | all-to-all | bytes 131072 | tf_op jit(solution)/shard_map/all_to_all | solution.py:22
  107.0 11.2 %all_to_all.54.got_ref = f32[32,8,128]{2,1,0:T(8,128)S(1)} all-to-all(f32[32,8,128]{2,1,0:T(8,128)S(1)} %broadcast_in_dim.24), channel_id=1, replica_groups=mesh['h'=4,'l'=4,'x'=4,'y'=4,'c'=2] {'x','y','c'}, dimensions={0} | all-to-all | bytes 262144 | tf_op jit(solution)/shard_map/all_to_all | solution.py:22
  118.7 15.7 %all_to_all.55.got_ref = f32[16,8,128]{2,1,0:T(8,128)S(1)} all-to-all(f32[16,8,128]{2,1,0:T(8,128)S(1)} %broadcast_in_dim.25), channel_id=1, replica_groups=mesh['h'=4,'l'=4,'x'=4,'y'=4,'c'=2] {'h','l'}, dimensions={0} | all-to-all | bytes 131072 | tf_op jit(solution)/shard_map/all_to_all | solution.py:22
  134.4 1.0 shard_map.56
  135.4 12.2 %all_to_all.56.got_ref = f32[32,16,128]{2,1,0:T(8,128)S(1)} all-to-all(f32[32,16,128]{2,1,0:T(8,128)S(1)} %broadcast_in_dim.26), channel_id=1, replica_groups=mesh['h'=4,'l'=4,'x'=4,'y'=4,'c'=2] {'x','y','c'}, dimensions={0} | all-to-all | bytes 524288 | tf_op jit(solution)/shard_map/all_to_all | solution.py:22
  147.6 1.9 shard_map.57
  149.6 33.6 %all_to_all.57 = f16[16,16,1024]{2,1,0:T(8,128)(2,1)S(1)} all-to-all(f16[16,16,1024]{2,1,0:T(8,128)(2,1)S(1)} %bitcast.15), channel_id=1, replica_groups=mesh['h'=4,'l'=4,'x'=4,'y'=4,'c'=2] {'h','l'}, dimensions={0} | all-to-all | bytes 1048576 | tf_op jit(solution)/shard_map/all_to_all | solution.py:242
  183.3 8.0 %all_to_all.58 = f32[4,4,1024]{2,1,0:T(4,128)S(1)} all-to-all(f32[4,4,1024]{2,1,0:T(4,128)S(1)} %broadcast_multiply_fusion), channel_id=1, replica_groups=mesh['h'=4,'l'=4,'x'=4,'y'=4,'c'=2] {'x'}, dimensions={0} | all-to-all | bytes 131072 | tf_op jit(solution)/shard_map/all_to_all | solution.py:244
  191.3 0.6 copy.11
  (20 shorter events, 2.1 us)
Async XLA Ops:
  11.3 42.4 %all-to-all-start.1 = ((bf16[16,16,1024]{2,1,0:T(8,128)(2,1)}), bf16[16,16,1024]{2,1,0:T(8,128)(2,1)S(1)}, u32[]{:S(2)}, u32[]{:S(2)}) async-start(bf16[16,16,1024]{2,1,0:T(8,128)(2,1)} %broadcast_in_dim.20), calls=%async_computation.1 | async-start | bytes 1048576 | tf_op jit(solution)/shard_map/all_to_all | solution.py:22
  27.6 10.8 %collective-permute-start = (bf16[256,512]{1,0:T(8,128)(2,1)S(1)}, bf16[256,512]{1,0:T(8,128)(2,1)S(1)}, u32[]{:S(2)}, u32[]{:S(2)}) collective-permute-start(bf16[256,512]{1,0:T(8,128)(2,1)S(1)} %shard_map.50), channel_id=1, source_target_pairs={{8,0},{16,8},{24,16},{0,24},{9,1},{17,9},{25,17},{1,25},{10,2},{18... | collective-permute-start | bytes 786440 | tf_op jit(solution)/shard_map/ppermute | solution.py:217
  30.7 12.4 %collective-permute-start.1 = (bf16[256,512]{1,0:T(8,128)(2,1)S(1)}, bf16[256,512]{1,0:T(8,128)(2,1)S(1)}, u32[]{:S(2)}, u32[]{:S(2)}) collective-permute-start(bf16[256,512]{1,0:T(8,128)(2,1)S(1)} %shard_map.50), channel_id=1, source_target_pairs={{16,0},{24,8},{0,16},{8,24},{17,1},{25,9},{1,17},{9,25},{18,2},{26... | collective-permute-start | bytes 786440 | tf_op jit(solution)/shard_map/ppermute | solution.py:217
  34.1 11.4 %collective-permute-start.2 = (bf16[256,512]{1,0:T(8,128)(2,1)S(1)}, bf16[256,512]{1,0:T(8,128)(2,1)S(1)}, u32[]{:S(2)}, u32[]{:S(2)}) collective-permute-start(bf16[256,512]{1,0:T(8,128)(2,1)S(1)} %shard_map.50), channel_id=1, source_target_pairs={{24,0},{0,8},{8,16},{16,24},{25,1},{1,9},{9,17},{17,25},{26,2},{2,... | collective-permute-start | bytes 786440 | tf_op jit(solution)/shard_map/ppermute | solution.py:217

commit v6 on v5

--- a/solution.py
+++ b/solution.py
@@ -58,9 +58,19 @@
     return jnp.concatenate([block[i : i + 1, :] for i in range(block.shape[0])], axis=1)
 
 
-def store_totals(out_ref, first, block):
+def put_totals(held, first, block):
+    row = lax.broadcasted_iota(jnp.int32, held.shape, 0)
     for i in range(TILE // LANES):
-        out_ref[pl.ds(first + i, 1), :] = row_totals(block[i * LANES : (i + 1) * LANES, :])
+        held = jnp.where(row == first + i, row_totals(block[i * LANES : (i + 1) * LANES, :]), held)
+    return held
+
+
+def over_tiles(step, ref, rows):
+    def body(i, held):
+        tile = pl.ds(pl.multiple_of(i * TILE, TILE), TILE)
+        return step(i * (TILE // LANES), tile, held)
+
+    return lax.fori_loop(0, ref.shape[0] // TILE, body, jnp.zeros((rows, LANES), jnp.float32))
 
 
 def masses_of(unit_ref, proto_ref, norm_ref, rows):
@@ -93,25 +103,24 @@
     scale = unfold(1.0 / (proto_count * jnp.sum(got_ref[...], axis=0)))
     half = out_ref.shape[0] // 2
 
-    @pl.loop(0, unit_ref.shape[0] // TILE)
-    def _(i):
-        rows = pl.ds(pl.multiple_of(i * TILE, TILE), TILE)
-        first = i * (TILE // LANES)
-        store_totals(out_ref, first, mass_ref[rows, :] * scale)
+    def step(first, rows, held):
         scores = scores_of(unit_ref, proto_ref, norm_ref, rows)
         spread = jnp.exp(scores)
         score_ref[rows, :] = scores
         spread_ref[rows, :] = spread
-        store_totals(out_ref, half + first, spread)
+        held = put_totals(held, first, mass_ref[rows, :] * scale)
+        return put_totals(held, half + first, spread)
+
+    out_ref[...] = over_tiles(step, mass_ref, 2 * half)
 
 
 def row_kernel(proto_count, mass_ref, got_ref, out_ref):
     scale = unfold(1.0 / (proto_count * jnp.sum(got_ref[...], axis=0)))
 
-    @pl.loop(0, mass_ref.shape[0] // TILE)
-    def _(i):
-        rows = pl.ds(pl.multiple_of(i * TILE, TILE), TILE)
-        store_totals(out_ref, i * (TILE // LANES), mass_ref[rows, :] * scale)
+    def step(first, rows, held):
+        return put_totals(held, first, mass_ref[rows, :] * scale)
+
+    out_ref[...] = over_tiles(step, mass_ref, out_ref.shape[0])
 
 
 def col_sums(scale, mass_ref):
@@ -142,22 +151,24 @@
     scale_ref[...] = scale
     half = out_ref.shape[0] // 2
 
-    @pl.loop(0, mass_ref.shape[0] // TILE)
-    def _(i):
-        rows = pl.ds(pl.multiple_of(i * TILE, TILE), TILE)
-        first = i * (TILE // LANES)
+    def step(first, rows, held):
         weighted = mass_ref[rows, :] * scale
-        store_totals(out_ref, first, weighted)
-        store_totals(out_ref, half + first, weighted * score_ref[rows, :])
-
-
-def grad_kernel(crop_count, here_ref, unit_ref, proto_ref, norm_ref, mass_ref, spread_ref, scale_ref, got_ref, total_ref, out_ref, back_ref, loss_ref, all_ref):
+        held = put_totals(held, first, weighted)
+        return put_totals(held, half + first, weighted * score_ref[rows, :])
+
+    out_ref[...] = over_tiles(step, mass_ref, 2 * half)
+
+
+def grad_kernel(crop_count, here_ref, unit_ref, proto_ref, norm_ref, mass_ref, spread_ref, scale_ref, got_ref, total_ref, out_ref, back_ref, loss_ref):
     sums = jnp.sum(got_ref[...], axis=0)
     totals = total_ref[...]
     half = totals.shape[0]
-    all_ref[...] = jnp.log(totals) - sums[half:] / sums[:half]
+    losses = jnp.log(totals) - sums[half:] / sums[:half]
     block = loss_ref.shape[0]
-    loss_ref[...] = all_ref[pl.ds(here_ref[0] * block, block), :]
+    loss = losses[:block]
+    for x in range(1, half // block):
+        loss = jnp.where(here_ref[0] == x, losses[x * block : (x + 1) * block], loss)
+    loss_ref[...] = loss
     bot = proto_ref.shape[0]
     by_row = 1.0 / sums[:half]
     by_total = 1.0 / totals
@@ -184,7 +195,7 @@
     back_ref[...] = 1.0 / (norm_ref[...] * (WIRE_SCALE * STUDENT_TEMP * crop_count))
 
 
-def call(kernel, outs, *args, reads, scalar=None, scratch=(), dtype=jnp.float32):
+def call(kernel, outs, *args, reads, scalar=None, dtype=jnp.float32):
     vmem = pl.BlockSpec(memory_space=pltpu.VMEM)
     specs = [vmem] * len(args)
     if scalar is not None:
@@ -194,7 +205,6 @@
         out_shape=[jax.ShapeDtypeStruct(shape, dtype) for shape in outs],
         in_specs=specs,
         out_specs=[vmem] * len(outs),
-        scratch_shapes=[pltpu.VMEM(shape, jnp.float32) for shape in scratch],
         compiler_params=pltpu.CompilerParams(vmem_limit_bytes=VMEM_LIMIT),
         cost_estimate=pl.CostEstimate(flops=reads, bytes_accessed=reads, transcendentals=0),
     )(*args)
@@ -237,7 +247,7 @@
     part, scale = share(functools.partial(cross_kernel, by_proto), [row_pair, line], mass, scores, gather(sums, Z, nz))
     grad, back, loss = share(
         functools.partial(grad_kernel, by_crop), [(bot, cols), line, (crops_in // LANES, LANES)], *held, mass, spread, scale, gather_head(part), totals,
-        scalar=here.astype(jnp.int32).reshape(1), scratch=[row_fold],
+        scalar=here.astype(jnp.int32).reshape(1),
     )
     wire = lax.all_to_all(grad.astype(jnp.float16).reshape(nz, nx * rows_in, cols), Z, 0, 0, tiled=True)
     total = jnp.sum(wire.astype(jnp.float32), axis=0) * back

time: 193 us -> 193 us (level)
  no operation moved by 1% of the time
where the time goes in v6:
time: 193 us; the launch traced here: 192 us
  blocking collectives  140 us (73%)
  starting transfers between devices  23.6 us (12%)
  waiting for transfers between devices  17.4 us (9%)
  Pallas kernels  7.74 us (4%)
    all_to_all x6, blocking collectives, gather(): return lax.all_to_all(copies, axes, 0, 0, tiled=True)  88.1 us
    all_to_all x1, blocking collectives, local(): lax.all_to_all(grad.astype(jnp.float16).reshape(nz, nx * rows_in, cols),...  33.6 us
    all_to_all x1, starting transfers between devices, gather(): return lax.all_to_all(copies, axes, 0, 0, tiled=True)  15.2 us
    all_to_all x1, blocking collectives, local(): lax.all_to_all(quarters, 'x', 0, 0, tiled=True).reshape(nx * rows_in, cols)  9.75 us
    ppermute x3, waiting for transfers between devices, local(): lax.ppermute(units, 'x', [((i + step) % nx, i) for i in range(nx)])  9.26 us
    ppermute x3, starting transfers between devices, local(): lax.ppermute(units, 'x', [((i + step) % nx, i) for i in range(nx)])  8.37 us
    all_to_all x1, waiting for transfers between devices, gather(): return lax.all_to_all(copies, axes, 0, 0, tiled=True)  8.12 us
    all_to_all x1, blocking collectives, local(): lax.all_to_all(total.reshape(nx, rows_in, cols), 'x', 0, 0, tiled=True)  8.04 us
  transfers between devices with their start and end apart: 4, of which 4 were waited for; matrix products, arithmetic and copies ran while one was open for 1% of the time, Pallas kernels for 0%

profile of v6, /device:TPU:32, one launch (start us, length us, event | category | flops | bytes accessed | tf_op | source)
XLA Modules:
  0.0 192.0 jit_solution(17565352825916118246)
XLA Ops:
  0.6 9.8 %all_to_all.50 = bf16[4,4,1024]{2,1,0:T(4,128)(2,1)S(1)} all-to-all(bf16[4,4,1024]{2,1,0:T(4,128)(2,1)} %bitcast.17), channel_id=1, replica_groups=mesh['h'=4,'l'=4,'x'=4,'y'=4,'c'=2] {'x'}, dimensions={0} | all-to-all | bytes 65536 | tf_op jit(solution)/shard_map/all_to_all | solution.py:231
  10.4 0.9 broadcast_in_dim.20
  11.3 15.2 %all-to-all-start.1 = ((bf16[16,16,1024]{2,1,0:T(8,128)(2,1)}), bf16[16,16,1024]{2,1,0:T(8,128)(2,1)S(1)}, u32[]{:S(2)}, u32[]{:S(2)}) async-start(bf16[16,16,1024]{2,1,0:T(8,128)(2,1)} %broadcast_in_dim.20), calls=%async_computation.1 | async-start | bytes 1048576 | tf_op jit(solution)/shard_map/all_to_all | solution.py:22
  26.5 1.0 pad_maximum_fusion.feat_ref
  27.6 3.1 %collective-permute-start = (bf16[256,512]{1,0:T(8,128)(2,1)S(1)}, bf16[256,512]{1,0:T(8,128)(2,1)S(1)}, u32[]{:S(2)}, u32[]{:S(2)}) collective-permute-start(bf16[256,512]{1,0:T(8,128)(2,1)S(1)} %shard_map.50), channel_id=1, source_target_pairs={{8,0},{16,8},{24,16},{0,24},{9,1},{17,9},{25,17},{1,25},{10,2},{18... | collective-permute-start | bytes 786440 | tf_op jit(solution)/shard_map/ppermute | solution.py:227
  30.7 3.4 %collective-permute-start.1 = (bf16[256,512]{1,0:T(8,128)(2,1)S(1)}, bf16[256,512]{1,0:T(8,128)(2,1)S(1)}, u32[]{:S(2)}, u32[]{:S(2)}) collective-permute-start(bf16[256,512]{1,0:T(8,128)(2,1)S(1)} %shard_map.50), channel_id=1, source_target_pairs={{16,0},{24,8},{0,16},{8,24},{17,1},{25,9},{1,17},{9,25},{18,2},{26... | collective-permute-start | bytes 786440 | tf_op jit(solution)/shard_map/ppermute | solution.py:227
  34.1 1.9 %collective-permute-start.2 = (bf16[256,512]{1,0:T(8,128)(2,1)S(1)}, bf16[256,512]{1,0:T(8,128)(2,1)S(1)}, u32[]{:S(2)}, u32[]{:S(2)}) collective-permute-start(bf16[256,512]{1,0:T(8,128)(2,1)S(1)} %shard_map.50), channel_id=1, source_target_pairs={{24,0},{0,8},{8,16},{16,24},{25,1},{1,9},{9,17},{17,25},{26,2},{2,... | collective-permute-start | bytes 786440 | tf_op jit(solution)/shard_map/ppermute | solution.py:227
  36.2 2.2 %collective-permute-done = bf16[256,512]{1,0:T(8,128)(2,1)S(1)} collective-permute-done((bf16[256,512]{1,0:T(8,128)(2,1)S(1)}, bf16[256,512]{1,0:T(8,128)(2,1)S(1)}, u32[]{:S(2)}, u32[]{:S(2)}) %collective-permute-start) | collective-permute-done | bytes 262176 | tf_op jit(solution)/shard_map/ppermute | solution.py:227
  38.4 4.7 %collective-permute-done.1 = bf16[256,512]{1,0:T(8,128)(2,1)S(1)} collective-permute-done((bf16[256,512]{1,0:T(8,128)(2,1)S(1)}, bf16[256,512]{1,0:T(8,128)(2,1)S(1)}, u32[]{:S(2)}, u32[]{:S(2)}) %collective-permute-start.1) | collective-permute-done | bytes 262176 | tf_op jit(solution)/shard_map/ppermute | solution.py:227
  43.1 2.4 %collective-permute-done.2 = bf16[256,512]{1,0:T(8,128)(2,1)S(1)} collective-permute-done((bf16[256,512]{1,0:T(8,128)(2,1)S(1)}, bf16[256,512]{1,0:T(8,128)(2,1)S(1)}, u32[]{:S(2)}, u32[]{:S(2)}) %collective-permute-start.2) | collective-permute-done | bytes 262176 | tf_op jit(solution)/shard_map/ppermute | solution.py:227
  45.6 8.1 %all-to-all-done.1 = bf16[16,16,1024]{2,1,0:T(8,128)(2,1)S(1)} async-done(((bf16[16,16,1024]{2,1,0:T(8,128)(2,1)}), bf16[16,16,1024]{2,1,0:T(8,128)(2,1)S(1)}, u32[]{:S(2)}, u32[]{:S(2)}) %all-to-all-start.1) | async-done | bytes 524320 | tf_op jit(solution)/shard_map/all_to_all | solution.py:22
  53.7 1.4 shard_map.51
  55.1 18.4 %all_to_all.51.got_ref = f32[16,8,128]{2,1,0:T(8,128)S(1)} all-to-all(f32[16,8,128]{2,1,0:T(8,128)S(1)} %broadcast_in_dim.21), channel_id=1, replica_groups=mesh['h'=4,'l'=4,'x'=4,'y'=4,'c'=2] {'h','l'}, dimensions={0} | all-to-all | bytes 131072 | tf_op jit(solution)/shard_map/all_to_all | solution.py:22
  73.5 1.8 shard_map.52
  75.3 14.4 %all_to_all.52.got_ref = f32[32,16,128]{2,1,0:T(8,128)S(1)} all-to-all(f32[32,16,128]{2,1,0:T(8,128)S(1)} %broadcast_in_dim.22), channel_id=1, replica_groups=mesh['h'=4,'l'=4,'x'=4,'y'=4,'c'=2] {'x','y','c'}, dimensions={0} | all-to-all | bytes 524288 | tf_op jit(solution)/shard_map/all_to_all | solution.py:22
  90.2 16.2 %all_to_all.53.got_ref = f32[16,8,128]{2,1,0:T(8,128)S(1)} all-to-all(f32[16,8,128]{2,1,0:T(8,128)S(1)} %broadcast_in_dim.23), channel_id=1, replica_groups=mesh['h'=4,'l'=4,'x'=4,'y'=4,'c'=2] {'h','l'}, dimensions={0} | all-to-all | bytes 131072 | tf_op jit(solution)/shard_map/all_to_all | solution.py:22
  107.0 11.2 %all_to_all.54.got_ref = f32[32,8,128]{2,1,0:T(8,128)S(1)} all-to-all(f32[32,8,128]{2,1,0:T(8,128)S(1)} %broadcast_in_dim.24), channel_id=1, replica_groups=mesh['h'=4,'l'=4,'x'=4,'y'=4,'c'=2] {'x','y','c'}, dimensions={0} | all-to-all | bytes 262144 | tf_op jit(solution)/shard_map/all_to_all | solution.py:22
  118.7 15.7 %all_to_all.55.got_ref = f32[16,8,128]{2,1,0:T(8,128)S(1)} all-to-all(f32[16,8,128]{2,1,0:T(8,128)S(1)} %broadcast_in_dim.25), channel_id=1, replica_groups=mesh['h'=4,'l'=4,'x'=4,'y'=4,'c'=2] {'h','l'}, dimensions={0} | all-to-all | bytes 131072 | tf_op jit(solution)/shard_map/all_to_all | solution.py:22
  134.4 1.0 shard_map.56
  135.4 12.2 %all_to_all.56.got_ref = f32[32,16,128]{2,1,0:T(8,128)S(1)} all-to-all(f32[32,16,128]{2,1,0:T(8,128)S(1)} %broadcast_in_dim.26), channel_id=1, replica_groups=mesh['h'=4,'l'=4,'x'=4,'y'=4,'c'=2] {'x','y','c'}, dimensions={0} | all-to-all | bytes 524288 | tf_op jit(solution)/shard_map/all_to_all | solution.py:22
  147.6 1.9 shard_map.57
  149.6 33.6 %all_to_all.57 = f16[16,16,1024]{2,1,0:T(8,128)(2,1)S(1)} all-to-all(f16[16,16,1024]{2,1,0:T(8,128)(2,1)S(1)} %bitcast.15), channel_id=1, replica_groups=mesh['h'=4,'l'=4,'x'=4,'y'=4,'c'=2] {'h','l'}, dimensions={0} | all-to-all | bytes 1048576 | tf_op jit(solution)/shard_map/all_to_all | solution.py:252
  183.3 8.0 %all_to_all.58 = f32[4,4,1024]{2,1,0:T(4,128)S(1)} all-to-all(f32[4,4,1024]{2,1,0:T(4,128)S(1)} %broadcast_multiply_fusion), channel_id=1, replica_groups=mesh['h'=4,'l'=4,'x'=4,'y'=4,'c'=2] {'x'}, dimensions={0} | all-to-all | bytes 131072 | tf_op jit(solution)/shard_map/all_to_all | solution.py:254
  191.3 0.6 copy.11
  (20 shorter events, 2.1 us)
Async XLA Ops:
  11.3 42.4 %all-to-all-start.1 = ((bf16[16,16,1024]{2,1,0:T(8,128)(2,1)}), bf16[16,16,1024]{2,1,0:T(8,128)(2,1)S(1)}, u32[]{:S(2)}, u32[]{:S(2)}) async-start(bf16[16,16,1024]{2,1,0:T(8,128)(2,1)} %broadcast_in_dim.20), calls=%async_computation.1 | async-start | bytes 1048576 | tf_op jit(solution)/shard_map/all_to_all | solution.py:22
  27.6 10.8 %collective-permute-start = (bf16[256,512]{1,0:T(8,128)(2,1)S(1)}, bf16[256,512]{1,0:T(8,128)(2,1)S(1)}, u32[]{:S(2)}, u32[]{:S(2)}) collective-permute-start(bf16[256,512]{1,0:T(8,128)(2,1)S(1)} %shard_map.50), channel_id=1, source_target_pairs={{8,0},{16,8},{24,16},{0,24},{9,1},{17,9},{25,17},{1,25},{10,2},{18... | collective-permute-start | bytes 786440 | tf_op jit(solution)/shard_map/ppermute | solution.py:227
  30.7 12.4 %collective-permute-start.1 = (bf16[256,512]{1,0:T(8,128)(2,1)S(1)}, bf16[256,512]{1,0:T(8,128)(2,1)S(1)}, u32[]{:S(2)}, u32[]{:S(2)}) collective-permute-start(bf16[256,512]{1,0:T(8,128)(2,1)S(1)} %shard_map.50), channel_id=1, source_target_pairs={{16,0},{24,8},{0,16},{8,24},{17,1},{25,9},{1,17},{9,25},{18,2},{26... | collective-permute-start | bytes 786440 | tf_op jit(solution)/shard_map/ppermute | solution.py:227
  34.1 11.4 %collective-permute-start.2 = (bf16[256,512]{1,0:T(8,128)(2,1)S(1)}, bf16[256,512]{1,0:T(8,128)(2,1)S(1)}, u32[]{:S(2)}, u32[]{:S(2)}) collective-permute-start(bf16[256,512]{1,0:T(8,128)(2,1)S(1)} %shard_map.50), channel_id=1, source_target_pairs={{24,0},{0,8},{8,16},{16,24},{25,1},{1,9},{9,17},{17,25},{26,2},{2,... | collective-permute-start | bytes 786440 | tf_op jit(solution)/shard_map/ppermute | solution.py:227

commit v7 on v6

--- a/solution.py
+++ b/solution.py
@@ -12,9 +12,9 @@
 STUDENT_TEMP = 0.1
 WIRE_SCALE = 32.0
 
-Z = ("h", "l")
-ZX = ("h", "l", "x")
-XYC = ("x", "y", "c")
+Z = "z"
+ZX = ("z", "x")
+XYC = ("x", "head")
 
 
 def gather(values, axes, size):
@@ -70,7 +70,7 @@
         tile = pl.ds(pl.multiple_of(i * TILE, TILE), TILE)
         return step(i * (TILE // LANES), tile, held)
 
-    return lax.fori_loop(0, ref.shape[0] // TILE, body, jnp.zeros((rows, LANES), jnp.float32))
+    return lax.fori_loop(0, ref.shape[0] // TILE, body, jnp.zeros((rows, LANES), jnp.float32), unroll=True)
 
 
 def masses_of(unit_ref, proto_ref, norm_ref, rows):
@@ -96,7 +96,7 @@
         return sums + jnp.sum(mass, axis=0, keepdims=True)
 
     steps = unit_ref.shape[0] // TILE
-    col_ref[...] = fold(lax.fori_loop(0, steps, step, jnp.zeros(norm_ref.shape, jnp.float32)))
+    col_ref[...] = fold(lax.fori_loop(0, steps, step, jnp.zeros(norm_ref.shape, jnp.float32), unroll=True))
 
 
 def first_row_kernel(proto_count, unit_ref, proto_ref, norm_ref, mass_ref, got_ref, out_ref, score_ref, spread_ref):
@@ -213,7 +213,7 @@
 def local(teacher_feat, student_feat, proto_v):
     rows_in, cols_in = proto_v.shape
     nx = lax.axis_size("x")
-    nz = lax.axis_size("h") * lax.axis_size("l")
+    nz = lax.axis_size("z")
     cols = cols_in // nx
     crop_count = teacher_feat.shape[0] * nz * nx
     proto_count = cols * 32
@@ -256,11 +256,11 @@
 
 
 def solution(mesh):
-    fine = Mesh(mesh.devices.reshape(4, 4, 4, 4, 2), ("h", "l", "x", "y", "c"))
+    fine = Mesh(mesh.devices.reshape(16, 4, 8), ("z", "x", "head"))
     return jax.shard_map(
         local,
         mesh=fine,
-        in_specs=(P(ZX, None), P(ZX, None), P(ZX, ("y", "c"))),
-        out_specs=(P(ZX, ("y", "c")), P(ZX)),
+        in_specs=(P(ZX, None), P(ZX, None), P(ZX, "head")),
+        out_specs=(P(ZX, "head"), P(ZX)),
         check_vma=False,
     )

time: 193 us -> 191 us (0.990)
  no operation moved by 1% of the time
where the time goes in v7:
time: 191 us
  blocking collectives  140 us (73%)
  starting transfers between devices  23.6 us (12%)
  waiting for transfers between devices  17.4 us (9%)
  Pallas kernels  6.42 us (3%)
    all_to_all x6, blocking collectives, gather(): return lax.all_to_all(copies, axes, 0, 0, tiled=True)  88.1 us
    all_to_all x1, blocking collectives, local(): lax.all_to_all(grad.astype(jnp.float16).reshape(nz, nx * rows_in, cols),...  33.6 us
    all_to_all x1, starting transfers between devices, gather(): return lax.all_to_all(copies, axes, 0, 0, tiled=True)  15.2 us
    all_to_all x1, blocking collectives, local(): lax.all_to_all(quarters, 'x', 0, 0, tiled=True).reshape(nx * rows_in, cols)  9.75 us
    ppermute x3, waiting for transfers between devices, local(): lax.ppermute(units, 'x', [((i + step) % nx, i) for i in range(nx)])  9.26 us
    ppermute x3, starting transfers between devices, local(): lax.ppermute(units, 'x', [((i + step) % nx, i) for i in range(nx)])  8.37 us
    all_to_all x1, waiting for transfers between devices, gather(): return lax.all_to_all(copies, axes, 0, 0, tiled=True)  8.12 us
    all_to_all x1, blocking collectives, local(): lax.all_to_all(total.reshape(nx, rows_in, cols), 'x', 0, 0, tiled=True)  8.02 us
  transfers between devices with their start and end apart: 4, of which 4 were waited for; matrix products, arithmetic and copies ran while one was open for 1% of the time, Pallas kernels for 0%

profile of v7, /device:TPU:32, one launch (start us, length us, event | category | flops | bytes accessed | tf_op | source)
XLA Modules:
  0.0 190.7 jit_solution(3891130182168023499)
XLA Ops:
  0.6 9.8 %all_to_all.50 = bf16[4,4,1024]{2,1,0:T(4,128)(2,1)S(1)} all-to-all(bf16[4,4,1024]{2,1,0:T(4,128)(2,1)} %bitcast.17), channel_id=1, replica_groups=mesh['z'=16,'x'=4,'head'=8] {'x'}, dimensions={0} | all-to-all | bytes 65536 | tf_op jit(solution)/shard_map/all_to_all | solution.py:231
  10.4 0.9 broadcast_in_dim.20
  11.3 15.2 %all-to-all-start.1 = ((bf16[16,16,1024]{2,1,0:T(8,128)(2,1)}), bf16[16,16,1024]{2,1,0:T(8,128)(2,1)S(1)}, u32[]{:S(2)}, u32[]{:S(2)}) async-start(bf16[16,16,1024]{2,1,0:T(8,128)(2,1)} %broadcast_in_dim.20), calls=%async_computation.1 | async-start | bytes 1048576 | tf_op jit(solution)/shard_map/all_to_all | solution.py:22
  26.5 1.0 pad_maximum_fusion.feat_ref
  27.6 3.1 %collective-permute-start = (bf16[256,512]{1,0:T(8,128)(2,1)S(1)}, bf16[256,512]{1,0:T(8,128)(2,1)S(1)}, u32[]{:S(2)}, u32[]{:S(2)}) collective-permute-start(bf16[256,512]{1,0:T(8,128)(2,1)S(1)} %shard_map.50), channel_id=1, source_target_pairs={{8,0},{16,8},{24,16},{0,24},{9,1},{17,9},{25,17},{1,25},{10,2},{18... | collective-permute-start | bytes 786440 | tf_op jit(solution)/shard_map/ppermute | solution.py:227
  30.7 3.4 %collective-permute-start.1 = (bf16[256,512]{1,0:T(8,128)(2,1)S(1)}, bf16[256,512]{1,0:T(8,128)(2,1)S(1)}, u32[]{:S(2)}, u32[]{:S(2)}) collective-permute-start(bf16[256,512]{1,0:T(8,128)(2,1)S(1)} %shard_map.50), channel_id=1, source_target_pairs={{16,0},{24,8},{0,16},{8,24},{17,1},{25,9},{1,17},{9,25},{18,2},{26... | collective-permute-start | bytes 786440 | tf_op jit(solution)/shard_map/ppermute | solution.py:227
  34.1 1.9 %collective-permute-start.2 = (bf16[256,512]{1,0:T(8,128)(2,1)S(1)}, bf16[256,512]{1,0:T(8,128)(2,1)S(1)}, u32[]{:S(2)}, u32[]{:S(2)}) collective-permute-start(bf16[256,512]{1,0:T(8,128)(2,1)S(1)} %shard_map.50), channel_id=1, source_target_pairs={{24,0},{0,8},{8,16},{16,24},{25,1},{1,9},{9,17},{17,25},{26,2},{2,... | collective-permute-start | bytes 786440 | tf_op jit(solution)/shard_map/ppermute | solution.py:227
  36.2 2.2 %collective-permute-done = bf16[256,512]{1,0:T(8,128)(2,1)S(1)} collective-permute-done((bf16[256,512]{1,0:T(8,128)(2,1)S(1)}, bf16[256,512]{1,0:T(8,128)(2,1)S(1)}, u32[]{:S(2)}, u32[]{:S(2)}) %collective-permute-start) | collective-permute-done | bytes 262176 | tf_op jit(solution)/shard_map/ppermute | solution.py:227
  38.4 4.7 %collective-permute-done.1 = bf16[256,512]{1,0:T(8,128)(2,1)S(1)} collective-permute-done((bf16[256,512]{1,0:T(8,128)(2,1)S(1)}, bf16[256,512]{1,0:T(8,128)(2,1)S(1)}, u32[]{:S(2)}, u32[]{:S(2)}) %collective-permute-start.1) | collective-permute-done | bytes 262176 | tf_op jit(solution)/shard_map/ppermute | solution.py:227
  43.1 2.4 %collective-permute-done.2 = bf16[256,512]{1,0:T(8,128)(2,1)S(1)} collective-permute-done((bf16[256,512]{1,0:T(8,128)(2,1)S(1)}, bf16[256,512]{1,0:T(8,128)(2,1)S(1)}, u32[]{:S(2)}, u32[]{:S(2)}) %collective-permute-start.2) | collective-permute-done | bytes 262176 | tf_op jit(solution)/shard_map/ppermute | solution.py:227
  45.6 8.1 %all-to-all-done.1 = bf16[16,16,1024]{2,1,0:T(8,128)(2,1)S(1)} async-done(((bf16[16,16,1024]{2,1,0:T(8,128)(2,1)}), bf16[16,16,1024]{2,1,0:T(8,128)(2,1)S(1)}, u32[]{:S(2)}, u32[]{:S(2)}) %all-to-all-start.1) | async-done | bytes 524320 | tf_op jit(solution)/shard_map/all_to_all | solution.py:22
  53.7 0.8 shard_map.51
  54.5 18.4 %all_to_all.51.got_ref = f32[16,8,128]{2,1,0:T(8,128)S(1)} all-to-all(f32[16,8,128]{2,1,0:T(8,128)S(1)} %broadcast_in_dim.21), channel_id=1, replica_groups=mesh['z'=16,'x'=4,'head'=8] {'z'}, dimensions={0} | all-to-all | bytes 131072 | tf_op jit(solution)/shard_map/all_to_all | solution.py:22
  72.9 1.3 shard_map.52
  74.3 14.5 %all_to_all.52.got_ref = f32[32,16,128]{2,1,0:T(8,128)S(1)} all-to-all(f32[32,16,128]{2,1,0:T(8,128)S(1)} %broadcast_in_dim.22), channel_id=1, replica_groups=mesh['z'=16,'x'=4,'head'=8] {'x','head'}, dimensions={0} | all-to-all | bytes 524288 | tf_op jit(solution)/shard_map/all_to_all | solution.py:22
  89.3 16.1 %all_to_all.53.got_ref = f32[16,8,128]{2,1,0:T(8,128)S(1)} all-to-all(f32[16,8,128]{2,1,0:T(8,128)S(1)} %broadcast_in_dim.23), channel_id=1, replica_groups=mesh['z'=16,'x'=4,'head'=8] {'z'}, dimensions={0} | all-to-all | bytes 131072 | tf_op jit(solution)/shard_map/all_to_all | solution.py:22
  105.8 11.2 %all_to_all.54.got_ref = f32[32,8,128]{2,1,0:T(8,128)S(1)} all-to-all(f32[32,8,128]{2,1,0:T(8,128)S(1)} %broadcast_in_dim.24), channel_id=1, replica_groups=mesh['z'=16,'x'=4,'head'=8] {'x','head'}, dimensions={0} | all-to-all | bytes 262144 | tf_op jit(solution)/shard_map/all_to_all | solution.py:22
  117.4 15.7 %all_to_all.55.got_ref = f32[16,8,128]{2,1,0:T(8,128)S(1)} all-to-all(f32[16,8,128]{2,1,0:T(8,128)S(1)} %broadcast_in_dim.25), channel_id=1, replica_groups=mesh['z'=16,'x'=4,'head'=8] {'z'}, dimensions={0} | all-to-all | bytes 131072 | tf_op jit(solution)/shard_map/all_to_all | solution.py:22
  133.1 0.9 shard_map.56
  134.1 12.2 %all_to_all.56.got_ref = f32[32,16,128]{2,1,0:T(8,128)S(1)} all-to-all(f32[32,16,128]{2,1,0:T(8,128)S(1)} %broadcast_in_dim.26), channel_id=1, replica_groups=mesh['z'=16,'x'=4,'head'=8] {'x','head'}, dimensions={0} | all-to-all | bytes 524288 | tf_op jit(solution)/shard_map/all_to_all | solution.py:22
  146.3 1.9 shard_map.57
  148.3 33.6 %all_to_all.57 = f16[16,16,1024]{2,1,0:T(8,128)(2,1)S(1)} all-to-all(f16[16,16,1024]{2,1,0:T(8,128)(2,1)S(1)} %bitcast.15), channel_id=1, replica_groups=mesh['z'=16,'x'=4,'head'=8] {'z'}, dimensions={0} | all-to-all | bytes 1048576 | tf_op jit(solution)/shard_map/all_to_all | solution.py:252
  182.0 8.0 %all_to_all.58 = f32[4,4,1024]{2,1,0:T(4,128)S(1)} all-to-all(f32[4,4,1024]{2,1,0:T(4,128)S(1)} %broadcast_multiply_fusion), channel_id=1, replica_groups=mesh['z'=16,'x'=4,'head'=8] {'x'}, dimensions={0} | all-to-all | bytes 131072 | tf_op jit(solution)/shard_map/all_to_all | solution.py:254
  190.0 0.6 copy.11
  (20 shorter events, 1.9 us)
Async XLA Ops:
  11.3 42.4 %all-to-all-start.1 = ((bf16[16,16,1024]{2,1,0:T(8,128)(2,1)}), bf16[16,16,1024]{2,1,0:T(8,128)(2,1)S(1)}, u32[]{:S(2)}, u32[]{:S(2)}) async-start(bf16[16,16,1024]{2,1,0:T(8,128)(2,1)} %broadcast_in_dim.20), calls=%async_computation.1 | async-start | bytes 1048576 | tf_op jit(solution)/shard_map/all_to_all | solution.py:22
  27.6 10.8 %collective-permute-start = (bf16[256,512]{1,0:T(8,128)(2,1)S(1)}, bf16[256,512]{1,0:T(8,128)(2,1)S(1)}, u32[]{:S(2)}, u32[]{:S(2)}) collective-permute-start(bf16[256,512]{1,0:T(8,128)(2,1)S(1)} %shard_map.50), channel_id=1, source_target_pairs={{8,0},{16,8},{24,16},{0,24},{9,1},{17,9},{25,17},{1,25},{10,2},{18... | collective-permute-start | bytes 786440 | tf_op jit(solution)/shard_map/ppermute | solution.py:227
  30.7 12.4 %collective-permute-start.1 = (bf16[256,512]{1,0:T(8,128)(2,1)S(1)}, bf16[256,512]{1,0:T(8,128)(2,1)S(1)}, u32[]{:S(2)}, u32[]{:S(2)}) collective-permute-start(bf16[256,512]{1,0:T(8,128)(2,1)S(1)} %shard_map.50), channel_id=1, source_target_pairs={{16,0},{24,8},{0,16},{8,24},{17,1},{25,9},{1,17},{9,25},{18,2},{26... | collective-permute-start | bytes 786440 | tf_op jit(solution)/shard_map/ppermute | solution.py:227
  34.1 11.4 %collective-permute-start.2 = (bf16[256,512]{1,0:T(8,128)(2,1)S(1)}, bf16[256,512]{1,0:T(8,128)(2,1)S(1)}, u32[]{:S(2)}, u32[]{:S(2)}) collective-permute-start(bf16[256,512]{1,0:T(8,128)(2,1)S(1)} %shard_map.50), channel_id=1, source_target_pairs={{24,0},{0,8},{8,16},{16,24},{25,1},{1,9},{9,17},{17,25},{26,2},{2,... | collective-permute-start | bytes 786440 | tf_op jit(solution)/shard_map/ppermute | solution.py:227

commit v8 on v7

--- a/solution.py
+++ b/solution.py
@@ -100,7 +100,7 @@
 
 
 def first_row_kernel(proto_count, unit_ref, proto_ref, norm_ref, mass_ref, got_ref, out_ref, score_ref, spread_ref):
-    scale = unfold(1.0 / (proto_count * jnp.sum(got_ref[...], axis=0)))
+    scale = unfold(1.0 / (proto_count * jnp.sum(got_ref[...].astype(jnp.float32), axis=0)))
     half = out_ref.shape[0] // 2
 
     def step(first, rows, held):
@@ -115,7 +115,7 @@
 
 
 def row_kernel(proto_count, mass_ref, got_ref, out_ref):
-    scale = unfold(1.0 / (proto_count * jnp.sum(got_ref[...], axis=0)))
+    scale = unfold(1.0 / (proto_count * jnp.sum(got_ref[...].astype(jnp.float32), axis=0)))
 
     def step(first, rows, held):
         return put_totals(held, first, mass_ref[rows, :] * scale)
@@ -136,18 +136,18 @@
 
 
 def first_col_kernel(crop_count, mass_ref, got_ref, out_ref, total_ref):
-    both = jnp.sum(got_ref[...], axis=0)
+    both = jnp.sum(got_ref[...].astype(jnp.float32), axis=0)
     half = both.shape[0] // 2
     total_ref[...] = both[half:]
     out_ref[...] = col_sums(1.0 / (crop_count * both[:half]), mass_ref)
 
 
 def col_kernel(crop_count, mass_ref, got_ref, out_ref):
-    out_ref[...] = col_sums(1.0 / (crop_count * jnp.sum(got_ref[...], axis=0)), mass_ref)
+    out_ref[...] = col_sums(1.0 / (crop_count * jnp.sum(got_ref[...].astype(jnp.float32), axis=0)), mass_ref)
 
 
 def cross_kernel(proto_count, mass_ref, score_ref, got_ref, out_ref, scale_ref):
-    scale = unfold(1.0 / (proto_count * jnp.sum(got_ref[...], axis=0)))
+    scale = unfold(1.0 / (proto_count * jnp.sum(got_ref[...].astype(jnp.float32), axis=0)))
     scale_ref[...] = scale
     half = out_ref.shape[0] // 2
 
@@ -160,7 +160,7 @@
 
 
 def grad_kernel(crop_count, here_ref, unit_ref, proto_ref, norm_ref, mass_ref, spread_ref, scale_ref, got_ref, total_ref, out_ref, back_ref, loss_ref):
-    sums = jnp.sum(got_ref[...], axis=0)
+    sums = jnp.sum(got_ref[...].astype(jnp.float32), axis=0)
     totals = total_ref[...]
     half = totals.shape[0]
     losses = jnp.log(totals) - sums[half:] / sums[:half]
@@ -239,10 +239,10 @@
     sums, norms, mass = share(teacher_kernel, [col_fold, line, whole], gathered, protos)
     held = gathered, protos, norms
     part, scores, spread = share(
-        functools.partial(first_row_kernel, by_proto), [row_pair, whole, whole], *held, mass, gather(sums, Z, nz)
+        functools.partial(first_row_kernel, by_proto), [row_pair, whole, whole], *held, mass, gather(sums.astype(jnp.bfloat16), Z, nz)
     )
     sums, totals = share(functools.partial(first_col_kernel, by_crop), [col_fold, row_fold], mass, gather_head(part))
-    (part,) = share(functools.partial(row_kernel, by_proto), [row_fold], mass, gather(sums, Z, nz))
+    (part,) = share(functools.partial(row_kernel, by_proto), [row_fold], mass, gather(sums.astype(jnp.bfloat16), Z, nz))
     (sums,) = share(functools.partial(col_kernel, by_crop), [col_fold], mass, gather_head(part))
     part, scale = share(functools.partial(cross_kernel, by_proto), [row_pair, line], mass, scores, gather(sums, Z, nz))
     grad, back, loss = share(

time: 191 us -> 190 us (level)
  no operation moved by 1% of the time
where the time goes in v8:
time: 190 us
  blocking collectives  139 us (73%)
  starting transfers between devices  23.6 us (12%)
  waiting for transfers between devices  17.4 us (9%)
  Pallas kernels  6.44 us (3%)
    all_to_all x6, blocking collectives, gather(): return lax.all_to_all(copies, axes, 0, 0, tiled=True)  87.2 us
    all_to_all x1, blocking collectives, local(): lax.all_to_all(grad.astype(jnp.float16).reshape(nz, nx * rows_in, cols),...  33.6 us
    all_to_all x1, starting transfers between devices, gather(): return lax.all_to_all(copies, axes, 0, 0, tiled=True)  15.2 us
    all_to_all x1, blocking collectives, local(): lax.all_to_all(quarters, 'x', 0, 0, tiled=True).reshape(nx * rows_in, cols)  9.75 us
    ppermute x3, waiting for transfers between devices, local(): lax.ppermute(units, 'x', [((i + step) % nx, i) for i in range(nx)])  9.26 us
    ppermute x3, starting transfers between devices, local(): lax.ppermute(units, 'x', [((i + step) % nx, i) for i in range(nx)])  8.37 us
    all_to_all x1, waiting for transfers between devices, gather(): return lax.all_to_all(copies, axes, 0, 0, tiled=True)  8.12 us
    all_to_all x1, blocking collectives, local(): lax.all_to_all(total.reshape(nx, rows_in, cols), 'x', 0, 0, tiled=True)  8.05 us
  transfers between devices with their start and end apart: 4, of which 4 were waited for; matrix products, arithmetic and copies ran while one was open for 1% of the time, Pallas kernels for 0%

profile of v8, /device:TPU:32, one launch (start us, length us, event | category | flops | bytes accessed | tf_op | source)
XLA Modules:
  0.0 189.7 jit_solution(13810121759766213224)
XLA Ops:
  0.6 9.8 %all_to_all.50 = bf16[4,4,1024]{2,1,0:T(4,128)(2,1)S(1)} all-to-all(bf16[4,4,1024]{2,1,0:T(4,128)(2,1)} %bitcast.17), channel_id=1, replica_groups=mesh['z'=16,'x'=4,'head'=8] {'x'}, dimensions={0} | all-to-all | bytes 65536 | tf_op jit(solution)/shard_map/all_to_all | solution.py:231
  10.4 0.9 broadcast_in_dim.20
  11.3 15.2 %all-to-all-start.1 = ((bf16[16,16,1024]{2,1,0:T(8,128)(2,1)}), bf16[16,16,1024]{2,1,0:T(8,128)(2,1)S(1)}, u32[]{:S(2)}, u32[]{:S(2)}) async-start(bf16[16,16,1024]{2,1,0:T(8,128)(2,1)} %broadcast_in_dim.20), calls=%async_computation.1 | async-start | bytes 1048576 | tf_op jit(solution)/shard_map/all_to_all | solution.py:22
  26.5 1.0 pad_maximum_fusion.feat_ref
  27.6 3.1 %collective-permute-start = (bf16[256,512]{1,0:T(8,128)(2,1)S(1)}, bf16[256,512]{1,0:T(8,128)(2,1)S(1)}, u32[]{:S(2)}, u32[]{:S(2)}) collective-permute-start(bf16[256,512]{1,0:T(8,128)(2,1)S(1)} %shard_map.50), channel_id=1, source_target_pairs={{8,0},{16,8},{24,16},{0,24},{9,1},{17,9},{25,17},{1,25},{10,2},{18... | collective-permute-start | bytes 786440 | tf_op jit(solution)/shard_map/ppermute | solution.py:227
  30.7 3.4 %collective-permute-start.1 = (bf16[256,512]{1,0:T(8,128)(2,1)S(1)}, bf16[256,512]{1,0:T(8,128)(2,1)S(1)}, u32[]{:S(2)}, u32[]{:S(2)}) collective-permute-start(bf16[256,512]{1,0:T(8,128)(2,1)S(1)} %shard_map.50), channel_id=1, source_target_pairs={{16,0},{24,8},{0,16},{8,24},{17,1},{25,9},{1,17},{9,25},{18,2},{26... | collective-permute-start | bytes 786440 | tf_op jit(solution)/shard_map/ppermute | solution.py:227
  34.1 1.9 %collective-permute-start.2 = (bf16[256,512]{1,0:T(8,128)(2,1)S(1)}, bf16[256,512]{1,0:T(8,128)(2,1)S(1)}, u32[]{:S(2)}, u32[]{:S(2)}) collective-permute-start(bf16[256,512]{1,0:T(8,128)(2,1)S(1)} %shard_map.50), channel_id=1, source_target_pairs={{24,0},{0,8},{8,16},{16,24},{25,1},{1,9},{9,17},{17,25},{26,2},{2,... | collective-permute-start | bytes 786440 | tf_op jit(solution)/shard_map/ppermute | solution.py:227
  36.2 2.2 %collective-permute-done = bf16[256,512]{1,0:T(8,128)(2,1)S(1)} collective-permute-done((bf16[256,512]{1,0:T(8,128)(2,1)S(1)}, bf16[256,512]{1,0:T(8,128)(2,1)S(1)}, u32[]{:S(2)}, u32[]{:S(2)}) %collective-permute-start) | collective-permute-done | bytes 262176 | tf_op jit(solution)/shard_map/ppermute | solution.py:227
  38.4 4.7 %collective-permute-done.1 = bf16[256,512]{1,0:T(8,128)(2,1)S(1)} collective-permute-done((bf16[256,512]{1,0:T(8,128)(2,1)S(1)}, bf16[256,512]{1,0:T(8,128)(2,1)S(1)}, u32[]{:S(2)}, u32[]{:S(2)}) %collective-permute-start.1) | collective-permute-done | bytes 262176 | tf_op jit(solution)/shard_map/ppermute | solution.py:227
  43.1 2.4 %collective-permute-done.2 = bf16[256,512]{1,0:T(8,128)(2,1)S(1)} collective-permute-done((bf16[256,512]{1,0:T(8,128)(2,1)S(1)}, bf16[256,512]{1,0:T(8,128)(2,1)S(1)}, u32[]{:S(2)}, u32[]{:S(2)}) %collective-permute-start.2) | collective-permute-done | bytes 262176 | tf_op jit(solution)/shard_map/ppermute | solution.py:227
  45.6 8.1 %all-to-all-done.1 = bf16[16,16,1024]{2,1,0:T(8,128)(2,1)S(1)} async-done(((bf16[16,16,1024]{2,1,0:T(8,128)(2,1)}), bf16[16,16,1024]{2,1,0:T(8,128)(2,1)S(1)}, u32[]{:S(2)}, u32[]{:S(2)}) %all-to-all-start.1) | async-done | bytes 524320 | tf_op jit(solution)/shard_map/all_to_all | solution.py:22
  53.7 0.8 shard_map.51
  54.5 18.0 %all_to_all.51.got_ref = bf16[16,8,128]{2,1,0:T(8,128)(2,1)S(1)} all-to-all(bf16[16,8,128]{2,1,0:T(8,128)(2,1)S(1)} %broadcast_in_dim.21), channel_id=1, replica_groups=mesh['z'=16,'x'=4,'head'=8] {'z'}, dimensions={0} | all-to-all | bytes 65536 | tf_op jit(solution)/shard_map/all_to_all | solution.py:22
  72.6 1.4 shard_map.52
  74.0 14.4 %all_to_all.52.got_ref = f32[32,16,128]{2,1,0:T(8,128)S(1)} all-to-all(f32[32,16,128]{2,1,0:T(8,128)S(1)} %broadcast_in_dim.22), channel_id=1, replica_groups=mesh['z'=16,'x'=4,'head'=8] {'x','head'}, dimensions={0} | all-to-all | bytes 524288 | tf_op jit(solution)/shard_map/all_to_all | solution.py:22
  88.9 15.1 %all_to_all.53.got_ref = bf16[16,8,128]{2,1,0:T(8,128)(2,1)S(1)} all-to-all(bf16[16,8,128]{2,1,0:T(8,128)(2,1)S(1)} %broadcast_in_dim.23), channel_id=1, replica_groups=mesh['z'=16,'x'=4,'head'=8] {'z'}, dimensions={0} | all-to-all | bytes 65536 | tf_op jit(solution)/shard_map/all_to_all | solution.py:22
  104.3 11.4 %all_to_all.54.got_ref = f32[32,8,128]{2,1,0:T(8,128)S(1)} all-to-all(f32[32,8,128]{2,1,0:T(8,128)S(1)} %broadcast_in_dim.24), channel_id=1, replica_groups=mesh['z'=16,'x'=4,'head'=8] {'x','head'}, dimensions={0} | all-to-all | bytes 262144 | tf_op jit(solution)/shard_map/all_to_all | solution.py:22
  116.1 16.1 %all_to_all.55.got_ref = f32[16,8,128]{2,1,0:T(8,128)S(1)} all-to-all(f32[16,8,128]{2,1,0:T(8,128)S(1)} %broadcast_in_dim.25), channel_id=1, replica_groups=mesh['z'=16,'x'=4,'head'=8] {'z'}, dimensions={0} | all-to-all | bytes 131072 | tf_op jit(solution)/shard_map/all_to_all | solution.py:22
  132.3 0.9 shard_map.56
  133.2 12.2 %all_to_all.56.got_ref = f32[32,16,128]{2,1,0:T(8,128)S(1)} all-to-all(f32[32,16,128]{2,1,0:T(8,128)S(1)} %broadcast_in_dim.26), channel_id=1, replica_groups=mesh['z'=16,'x'=4,'head'=8] {'x','head'}, dimensions={0} | all-to-all | bytes 524288 | tf_op jit(solution)/shard_map/all_to_all | solution.py:22
  145.4 1.9 %shard_map.57 = (f32[256,1024]{1,0:T(8,128)S(1)}, f32[1,1024]{1,0:T(1,128)S(1)}, f32[2,128]{1,0:T(2,128)}) custom-call(s32[1]{0:T(128)} %bitcast.here_ref, bf16[1024,512]{1,0:T(8,128)(2,1)S(1)} %constant_dynamic-update-slice_fusion.unit_ref, bf16[256,1024]{1,0:T(8,128)(2,1)S(1)} %bitcast.13, f32[1,1024]{1,0:T(1,128)S(1)} %get-tuple-element.15.norm_ref, ...), custom_call_target="tpu_custom_call" | custom-call | flops 4194304 | bytes 4194304 | tf_op jit(solution)/shard_map/pallas_call | solution.py:203
  147.4 33.6 %all_to_all.57 = f16[16,16,1024]{2,1,0:T(8,128)(2,1)S(1)} all-to-all(f16[16,16,1024]{2,1,0:T(8,128)(2,1)S(1)} %bitcast.15), channel_id=1, replica_groups=mesh['z'=16,'x'=4,'head'=8] {'z'}, dimensions={0} | all-to-all | bytes 1048576 | tf_op jit(solution)/shard_map/all_to_all | solution.py:252
  181.1 8.0 %all_to_all.58 = f32[4,4,1024]{2,1,0:T(4,128)S(1)} all-to-all(f32[4,4,1024]{2,1,0:T(4,128)S(1)} %broadcast_multiply_fusion), channel_id=1, replica_groups=mesh['z'=16,'x'=4,'head'=8] {'x'}, dimensions={0} | all-to-all | bytes 131072 | tf_op jit(solution)/shard_map/all_to_all | solution.py:254
  189.1 0.6 copy.11
  (22 shorter events, 1.9 us)
Async XLA Ops:
  11.3 42.4 %all-to-all-start.1 = ((bf16[16,16,1024]{2,1,0:T(8,128)(2,1)}), bf16[16,16,1024]{2,1,0:T(8,128)(2,1)S(1)}, u32[]{:S(2)}, u32[]{:S(2)}) async-start(bf16[16,16,1024]{2,1,0:T(8,128)(2,1)} %broadcast_in_dim.20), calls=%async_computation.1 | async-start | bytes 1048576 | tf_op jit(solution)/shard_map/all_to_all | solution.py:22
  27.6 10.8 %collective-permute-start = (bf16[256,512]{1,0:T(8,128)(2,1)S(1)}, bf16[256,512]{1,0:T(8,128)(2,1)S(1)}, u32[]{:S(2)}, u32[]{:S(2)}) collective-permute-start(bf16[256,512]{1,0:T(8,128)(2,1)S(1)} %shard_map.50), channel_id=1, source_target_pairs={{8,0},{16,8},{24,16},{0,24},{9,1},{17,9},{25,17},{1,25},{10,2},{18... | collective-permute-start | bytes 786440 | tf_op jit(solution)/shard_map/ppermute | solution.py:227
  30.7 12.4 %collective-permute-start.1 = (bf16[256,512]{1,0:T(8,128)(2,1)S(1)}, bf16[256,512]{1,0:T(8,128)(2,1)S(1)}, u32[]{:S(2)}, u32[]{:S(2)}) collective-permute-start(bf16[256,512]{1,0:T(8,128)(2,1)S(1)} %shard_map.50), channel_id=1, source_target_pairs={{16,0},{24,8},{0,16},{8,24},{17,1},{25,9},{1,17},{9,25},{18,2},{26... | collective-permute-start | bytes 786440 | tf_op jit(solution)/shard_map/ppermute | solution.py:227
  34.1 11.4 %collective-permute-start.2 = (bf16[256,512]{1,0:T(8,128)(2,1)S(1)}, bf16[256,512]{1,0:T(8,128)(2,1)S(1)}, u32[]{:S(2)}, u32[]{:S(2)}) collective-permute-start(bf16[256,512]{1,0:T(8,128)(2,1)S(1)} %shard_map.50), channel_id=1, source_target_pairs={{24,0},{0,8},{8,16},{16,24},{25,1},{1,9},{9,17},{17,25},{26,2},{2,... | collective-permute-start | bytes 786440 | tf_op jit(solution)/shard_map/ppermute | solution.py:227
